TPU v7x, 32 devices: a whole 2x2x4 slice. The times are simulated.
32 devices in a mesh: space: 16 (over z, y, x), rep: 2 (over core).
Axes of the slice: x: 2, y: 2, z: 4, core: 2. Of those that a mesh axis runs over, the one named last changes fastest.
Arguments:
- acts: bfloat16 [384, 512, 128], P(('space', 'rep')), may hold values from -6 to 6
- preact: bfloat16 [384, 512, 128], P(('space', 'rep')), may hold values from -8 to 8
- cotangent: bfloat16 [384, 512, 128], P(('space', 'rep')), may hold values from -6 to 6
- filt: bfloat16 [3456, 128], P('space', 'rep'), may hold values from -0.109375 to 0.109375
- counts: int32 [32], replicated, may hold values from 1 to 12, as said below
- neighbors: int32 [384, 27], P(('space', 'rep')), may hold values from 0 to 384, as said below
Outputs:
- input_grad: bfloat16 [384, 512, 128], P(('space', 'rep'))
- filt_grad: float32 [3456, 128], P('space', 'rep')
Inputs may be any that keep to these rules, and one draw needn't show every extreme that they name: counts[d] is the number of live bricks of device d, which fill its first slots; counts[d] + counts[d xor 1] <= 16, where d xor 1 is the other core of the same chip; in every draw some device holds 12 bricks and its partner 2 * 8 - 12. Brick n = d * 12 + s sits in slab d of the brick grid at one of 5 x 5 places, slot 0 of every device at the middle place; neighbors[n, k] is the index of the live brick at offset off_k (first component along the slabs, so it lies on device d - 1, d or d + 1) from that place, or 384 where there is none, also for bricks that are not live.
All inputs are finite; a program needn't handle non-finite values.
Results may differ from a plain program's by a relative error of at most 0.0049.
Values may be sent and summed in bfloat16 or wider, within the bound.
No kernel may reach another device: no remote copies, remote signals or barrier semaphores. Data moves between devices by JAX's collectives and lax.ppermute only.
A program may use at most 128 MiB of HBM per device.

v0:
```python
import functools
import math

import jax
import jax.numpy as jnp
from jax import lax
from jax.experimental import pallas as pl
from jax.experimental.pallas import tpu as pltpu
from jax.sharding import PartitionSpec as P

f32 = jnp.float32
bf16 = jnp.bfloat16
AXES = ("space", "rep")
LANES = 128


def silu_slope(values):
    sigma = jax.nn.sigmoid(values)
    return sigma * (1.0 + values * (1.0 - sigma))


def gated(preact, cotangent):
    return (cotangent.astype(f32) * silu_slope(preact.astype(f32))).astype(bf16)


def with_neighbour(x, first):
    count = lax.axis_size(AXES)
    pairs = []
    for low in range(first, count - 1, 2):
        pairs += [(low, low + 1), (low + 1, low)]
    return lax.ppermute(x, AXES, pairs)


def swapped(x, axis, mask):
    count = lax.axis_size(axis)
    return lax.ppermute(x, axis, [(i, i ^ mask) for i in range(count)])


def steps_of(count, most):
    out, unit = [], 1
    while unit < count:
        members = min(most, count // unit)
        out.append((unit, members))
        unit *= members
    return out


def loop(first, last, do):
    def body(index, carry):
        do(index)
        return carry

    lax.fori_loop(first, last, body, 0)


def neighbour_slots(read, brick, layer, position, slots, total, live, offset=0):
    base = (position + (layer - 1)) * slots - offset
    row_of = jnp.clip(brick, 0, slots - 1)
    table = []
    for dy in range(3):
        row = []
        for dz in range(3):
            value = read(row_of, layer * 9 + dy * 3 + dz)
            row.append(jnp.where((value >= total) | (brick >= live), slots, value - base))
        table.append(row)
    return table


def reader(ref):
    return lambda row, tap: ref[row, tap]


def shares(counts, slots):
    position = lax.axis_index(AXES)
    own, partner = counts[position], counts[position ^ 1]
    most = slots // 3
    gives = jnp.minimum(lax.div(jnp.maximum(own - partner, 0), 2), most)
    takes = jnp.minimum(lax.div(jnp.maximum(partner - own, 0), 2), most)
    return own, partner, gives, takes


def first_share(keep, takes):
    return jnp.maximum(2 * lax.div(keep + takes + 3, 4), takes)


def fill(unrolled, row, source, plane, table, side):
    def lines(dz):
        below = source[table[0][dz], plane, side - 1 : side]
        centre = source[table[1][dz], plane]
        above = source[table[2][dz], plane, 0:1]
        return jnp.concatenate([below, centre, above], axis=0)

    left, centre, right = lines(0), lines(1), lines(2)
    at = lax.broadcasted_iota(jnp.int32, centre.shape, 1)
    ahead = pltpu.roll(jnp.where(at == 0, right, centre), side - 1, 1)
    behind = pltpu.roll(jnp.where(at == side - 1, left, centre), 1, 1)
    for oy in range(3):
        for oz, values in enumerate((ahead, centre, behind)):
            column = (oy * 3 + oz) * LANES
            part = values[2 - oy : 2 - oy + side].reshape(side * side, LANES)
            unrolled[row : row + side * side, column : column + LANES] = part.astype(bf16)


def fill_brick(unrolled, field, table, side):
    for plane in range(side):
        fill(unrolled, plane * side * side, field, plane, table, side)


def gate_kernel(
    side, acts_far, preact_far, cotangent_far, grads, near, far, acts,
    preact, cotangent, sems,
):
    rep = lax.axis_index("rep")
    slots = preact.shape[0]
    area = side * side
    middle = preact.shape[1] // 2
    loads = [loader(preact_far, preact, sems, 0), loader(cotangent_far, cotangent, sems, 1)]
    load_acts = loader(acts_far, acts, sems, 2)

    def start(brick):
        for load in loads:
            load(brick).start()

    loop(0, slots, start)
    loop(0, slots, lambda brick: load_acts(brick).start())

    def gate(brick):
        for load in loads:
            load(brick).wait()
        ends = []
        for part in range(2):
            rows = pl.ds(part * middle, middle)
            values = gated(preact[brick, rows], cotangent[brick, rows])
            ends.append(values[:area] if part == 0 else values[-area:])
            grads[brick, rows] = values
        near[brick] = jnp.where(rep == 0, ends[1], ends[0])
        far[brick] = jnp.where(rep == 0, ends[0], ends[1])

    loop(0, slots, gate)
    loop(0, slots, lambda brick: load_acts(brick).wait())


def filter_step(side, first, last, table_of, acts, field, sums, unrolled, turned):
    area = side * side

    def prepare(brick, turn):
        fill_brick(unrolled[turn], field, table_of(brick), side)
        block = acts[jnp.minimum(brick, last - 1)]
        none = jnp.zeros((area, LANES), bf16)
        turned[turn][0:LANES] = jnp.concatenate([none, block[:-area]], axis=0).T
        turned[turn][LANES : 2 * LANES] = block.T
        turned[turn][2 * LANES :] = jnp.concatenate([block[area:], none], axis=0).T

    def multiply(turn):
        sums[...] += jnp.dot(turned[turn][...], unrolled[turn][...], preferred_element_type=f32)

    @pl.when(last > first)
    def _():
        prepare(first, 0)

        def pair(step, carry):
            brick = first + 2 * step
            prepare(brick + 1, 1)
            multiply(0)
            prepare(brick + 2, 0)
            multiply(1)
            return carry

        lax.fori_loop(0, lax.div(last - first + 1, 2), pair, 0)


def loader(source, target, sems, row):
    def load(brick):
        return pltpu.make_async_copy(source.at[brick], target.at[brick], sems.at[row, brick])

    return load


def inner_kernel(
    side, counts, neighbors, other_neighbors, acts, other_acts, grads, other_grads, after,
    sums, field, token, even, odd, even_turned, odd_turned,
):
    token[...] = jnp.zeros(token.shape, f32)
    position = lax.axis_index(AXES)
    slots = neighbors.shape[0]
    total = slots * counts.shape[0]
    own, partner, gives, takes = shares(counts, slots)

    def widen(brick, carry):
        field[brick] = grads[brick].astype(f32).reshape(field.shape[1:])
        return carry

    def widen_other(brick, carry):
        field[slots + 1 + brick] = other_grads[brick].astype(f32).reshape(field.shape[1:])
        return carry

    lax.fori_loop(0, own, widen, 0)
    lax.fori_loop(0, jnp.where(takes > 0, partner, 0), widen_other, 0)
    field[slots] = jnp.zeros(field.shape[1:], f32)
    sums[...] = jnp.zeros(sums.shape, f32)
    scratch = (even, odd), (even_turned, odd_turned)
    keep = own - gives

    def table(brick):
        return neighbour_slots(reader(neighbors), brick, 1, position, slots, total, keep)

    def other_table(brick):
        return neighbour_slots(
            reader(other_neighbors), brick, 1, position ^ 1, slots, total, partner, slots + 1
        )

    filter_step(side, 0, keep, table, acts, field, sums, *scratch)
    filter_step(side, partner - takes, partner, other_table, other_acts, field, sums, *scratch)


def outer_kernel(
    side, rows, half, counts, neighbors, acts, other_grads, far, sums, after,
    mine, sent, low_field, high_field, unrolled, table_sum,
):
    position = lax.axis_index(AXES)
    rep = lax.axis_index("rep")
    slots = far.shape[0]
    total = slots * counts.shape[0]
    area = side * side
    live = counts[position]
    extra = []
    for layer, field, plane in ((0, low_field, 0), (2, high_field, side - 1)):
        start = (side - 1) * area if layer == 0 else 0
        edge = jnp.where(rep == layer // 2, far[...], other_grads[:, start : start + area])
        field[0:slots] = edge.astype(f32).reshape(field[0:slots].shape)
        field[slots] = jnp.zeros(field.shape[1:], f32)
        for brick in range(slots):
            table = neighbour_slots(reader(neighbors), brick, layer, position, slots, total, live)
            fill(unrolled, brick * area, field, 0, table, side)
        flat = acts[:, plane * area : (plane + 1) * area].reshape(slots * area, LANES)
        extra.append(jnp.dot(flat.T, unrolled[...], preferred_element_type=f32))
    adds = (extra[1], None, extra[0])
    for ox in range(3):
        for column in range(9):
            tile = (slice(ox * LANES, (ox + 1) * LANES), slice(column * LANES, (column + 1) * LANES))
            part = sums[tile]
            if adds[ox] is not None:
                part = part + adds[ox][:, tile[1]]
            start = (ox * 9 + column) * LANES
            table_sum[start : start + LANES] = part
    count = 27 * LANES
    table_sum[count:] = jnp.zeros((table_sum.shape[0] - count, LANES), f32)
    blocks, padded = mine.shape[0], mine.shape[1]
    lane = lax.broadcasted_iota(jnp.int32, (padded, LANES), 1)
    for block in range(blocks):
        top = table_sum[block * rows : block * rows + padded]
        bottom = table_sum[block * rows + half : block * rows + half + padded]
        top_turned, bottom_turned = pltpu.roll(top, LANES // 2, 1), pltpu.roll(bottom, LANES // 2, 1)
        first = jnp.where(lane < LANES // 2, top, bottom_turned)
        second = jnp.where(lane < LANES // 2, top_turned, bottom)
        mine[block] = jnp.where(rep == 0, first, second)
        start = block * padded
        sent[start : start + padded] = jnp.where(rep == 0, second, first).astype(bf16)
    start = blocks * padded
    sent[start : start + slots * area] = far[...].reshape(slots * area, LANES)


def reduce_kernel(unit, members, arrivals, passes, waits, held, *refs):
    arrived, refs = refs[:arrivals], refs[arrivals + passes + waits :]
    keep, sends = refs[0], refs[1:members]
    own = lax.rem(lax.div(lax.axis_index("space"), unit), members)
    for block in range(keep.shape[0]):
        for member in range(members):
            at = block * members + (own ^ member)
            value = held[at]
            for ref in arrived:
                if len(ref.shape) == 3:
                    part = ref[at]
                else:
                    padded = keep.shape[1]
                    part = ref[pl.ds(pl.multiple_of(at * padded, 16), padded)]
                value = value + part.astype(f32)
            if member == 0:
                keep[block] = value
            else:
                sends[member - 1][block] = value.astype(bf16)


def stack_kernel(members, others, *refs):
    out = refs[members + others]
    for member, ref in enumerate(refs[:members]):
        for block in range(ref.shape[0]):
            out[block * members + member] = ref[block]


def last_kernel(scale, half, arrivals, held, *refs):
    arrived, out = refs[:arrivals], refs[-1]
    value = held[0]
    for ref in arrived:
        value = value + ref[0].astype(f32)
    turned = (value * scale).T
    columns, rows = out.shape
    out[:, :half] = turned[:columns, :half]
    out[:, half:] = turned[columns:, : rows - half]


def filter_kernel(held, arrived, after, filt, wide):
    space, rep = lax.axis_index("space"), lax.axis_index("rep")
    blocks, columns, rows = held.shape
    for block in range(blocks):
        own = held[block ^ space].astype(f32)
        others = arrived[block ^ space].astype(f32)
        at = slice(block * rows, (block + 1) * rows)
        wide[:columns, at] = jnp.where(rep == 0, own, others)
        wide[columns:, at] = jnp.where(rep == 0, others, own)
    for ox in range(3):
        for column in range(9):
            at = (ox * 9 + column) * LANES
            block = wide[:, at : at + LANES].astype(bf16)
            filt[column * LANES : (column + 1) * LANES, ox * LANES : (ox + 1) * LANES] = block


def input_step(side, first, last, table_of, field, low, high, filt, staged, scratch, at_step):
    even, odd, product = scratch
    unrolled = (even, odd)
    area = side * side
    voxels = area * side

    def prepare(brick, turn):
        fill(unrolled[turn], 0, low, 0, table_of(brick, 0), side)
        table = table_of(brick, 1)
        for plane in range(side):
            fill(unrolled[turn], (plane + 1) * area, field, plane, table, side)
        fill(unrolled[turn], (side + 1) * area, high, 0, table_of(brick, 2), side)

    def finish(brick, turn):
        product[...] = jnp.dot(unrolled[turn][...], filt[...], preferred_element_type=f32)
        values = product[2 * area :, 0:LANES] + product[area : area + voxels, LANES : 2 * LANES]
        values = values + product[0:voxels, 2 * LANES :]
        staged[brick - first] = values.astype(bf16)

    @pl.when(last > first)
    def _():
        prepare(first, 0)

        def pair(step, carry):
            brick = first + 2 * step
            at_step(step)
            prepare(brick + 1, 1)
            finish(brick, 0)
            prepare(brick + 2, 0)
            finish(brick + 1, 1)
            return carry

        lax.fori_loop(0, lax.div(last - first + 1, 2), pair, 0)


def sent_early(first, last):
    return jnp.maximum(lax.div(jnp.maximum(last - first, 0) + 1, 2) - 1, 0) * 2


def input_first_kernel(
    side, start, counts, neighbors, other_neighbors, field, low, high, near, arrived, filt, after,
    give, token, edge_low, edge_high, even, odd, product,
):
    token[...] = jnp.zeros(token.shape, f32)
    position = lax.axis_index(AXES)
    rep = lax.axis_index("rep")
    slots = near.shape[0]
    total = slots * counts.shape[0]
    own, partner, gives, takes = shares(counts, slots)
    keep = own - gives
    last = jnp.minimum(first_share(keep, takes), keep + takes)

    def table_of(item, layer):
        taken = item < takes
        brick = jnp.where(taken, partner - takes + item, item - takes)
        whose = jnp.where(taken, position ^ 1, position)
        offset = jnp.where(taken, slots + 1, 0)
        live = jnp.where(item < last, slots, 0)

        def read(row, tap):
            return jnp.where(taken, other_neighbors[row, tap], neighbors[row, tap])

        return neighbour_slots(read, brick, layer, whose, slots, total, live, offset)

    near_wide = near[...].astype(f32).reshape(low[0:slots].shape)
    far_rows = arrived[start : start + slots * side * side]
    far_wide = far_rows.astype(f32).reshape(low[0:slots].shape)
    edge_low[0 : slots + 1] = low[...]
    edge_high[0 : slots + 1] = high[...]
    edge_low[slots + 1 :] = jnp.where(rep == 0, near_wide, far_wide)
    edge_high[slots + 1 :] = jnp.where(rep == 0, far_wide, near_wide)
    scratch = even, odd, product
    input_step(
        side, 0, last, table_of, field, edge_low, edge_high, filt, give, scratch, lambda step: None
    )


def input_rest_kernel(
    side, counts, neighbors, field, low, high, filt, done, returned, after,
    out, token, staged, none, even, odd, product, sems,
):
    token[...] = jnp.zeros(token.shape, f32)
    position = lax.axis_index(AXES)
    slots = out.shape[0]
    total = slots * counts.shape[0]
    own, partner, gives, takes = shares(counts, slots)
    keep = own - gives
    first = jnp.minimum(first_share(keep, takes) - takes, keep)
    none[...] = jnp.zeros(none.shape, bf16)

    def table_of(brick, layer):
        return neighbour_slots(reader(neighbors), brick, layer, position, slots, total, keep)

    def copy(source, brick):
        return pltpu.make_async_copy(source, out.at[brick], sems.at[brick])

    loop(0, first, lambda brick: copy(done.at[takes + brick], brick).start())
    loop(keep, own, lambda brick: copy(returned.at[brick - keep], brick).start())
    loop(own, slots, lambda brick: copy(none, brick).start())

    def send(member):
        copy(staged.at[member], first + member).start()

    def at_step(step):
        @pl.when(step > 0)
        def _():
            send(2 * step - 2)
            send(2 * step - 1)

    scratch = even, odd, product
    input_step(side, first, keep, table_of, field, low, high, filt, staged, scratch, at_step)
    loop(sent_early(first, keep), keep - first, send)
    loop(0, slots, lambda brick: copy(none, brick).wait())


def call(kernel, outs, specs, scratch, flops, out_specs=None, aliases=None, limit=24 << 20):
    places = {"s": pltpu.SMEM, "v": pltpu.VMEM, "a": pl.ANY}
    whole = pl.BlockSpec(memory_space=pltpu.VMEM)
    return pl.pallas_call(
        kernel,
        out_shape=outs,
        in_specs=[pl.BlockSpec(memory_space=places[place]) for place in specs],
        out_specs=out_specs or jax.tree.map(lambda _: whole, outs),
        scratch_shapes=scratch,
        input_output_aliases=aliases or {},
        cost_estimate=pl.CostEstimate(flops=flops, bytes_accessed=1 << 20, transcendentals=0),
        compiler_params=pltpu.CompilerParams(vmem_limit_bytes=limit),
    )


def on_device(acts, preact, cotangent, filt, counts, neighbors):
    slots, voxels, channels = acts.shape
    side = round(voxels ** (1 / 3))
    area = side * side
    spaces = lax.axis_size("space")
    devices = lax.axis_size(AXES)
    rows = filt.shape[0]
    half = (rows + 1) // 2
    padded = -(-half // 16) * 16
    steps = steps_of(spaces, 4)
    flops = 2 * 27 * voxels * channels * channels * slots

    def like(shape, kind):
        return jax.ShapeDtypeStruct(shape, kind)

    shards = filt.T[None]
    low = min(4, spaces)
    gather = [(low * unit, members) for unit, members in reversed(steps_of(spaces // low, 2))]
    gather.append((1, low))

    def gather_start(number, own):
        unit, members = gather[number]
        return [own] + [swapped(own, "space", unit * m) for m in range(1, members)]

    def gather_finish(arrived, after=(), passed=()):
        own = arrived[0]
        members = len(arrived)
        waits = len(after) + len(passed)
        whole, anywhere = (pl.BlockSpec(memory_space=place) for place in (pltpu.VMEM, pl.ANY))
        return call(
            functools.partial(stack_kernel, members, waits),
            (like((members * own.shape[0],) + own.shape[1:], bf16),)
            + tuple(like(x.shape, x.dtype) for x in passed),
            "v" * members + "a" * waits,
            [],
            10**6,
            out_specs=(whole,) + (anywhere,) * len(passed),
            aliases={members + len(after) + i: 1 + i for i in range(len(passed))},
        )(*arrived, *after, *passed)

    field_shape = like((2 * slots + 1, side, side, side, channels), f32)
    edge_shape = like((slots + 1, 1, side, side, channels), f32)
    sums_shape = like((3 * channels, 9 * channels), f32)
    plane_shape = like((slots, area, channels), bf16)
    buffers = [pltpu.VMEM((voxels, 9 * channels), bf16)] * 2
    turned = [pltpu.VMEM((3 * channels, voxels), bf16)] * 2
    on_the_way = gather_start(0, shards)
    other_neighbors = swapped(neighbors, "rep", 1)
    grads, near, far, acts = call(
        functools.partial(gate_kernel, side),
        (like(acts.shape, bf16), plane_shape, plane_shape, like(acts.shape, bf16)),
        "aaa",
        [pltpu.VMEM(acts.shape, bf16)] * 2 + [pltpu.SemaphoreType.DMA((3, slots))],
        flops // 5,
        limit=50 << 20,
    )(acts, preact, cotangent)
    shards, grads, acts, far = gather_finish(on_the_way, passed=(grads, acts, far))
    other_grads, other_acts = swapped(grads, "rep", 1), swapped(acts, "rep", 1)
    far = with_neighbour(far, 1)
    for number in range(1, len(gather) - 1):
        (shards,) = gather_finish(gather_start(number, shards))
    on_the_way = gather_start(len(gather) - 1, shards)
    sums, field, token = call(
        functools.partial(inner_kernel, side),
        (sums_shape, field_shape, like((8, LANES), f32)),
        "sssvvvva",
        buffers + turned,
        flops,
    )(counts, neighbors, other_neighbors, acts, other_acts, grads, other_grads, shards)
    other_far = swapped(far, "rep", 1)
    (shards,) = gather_finish(on_the_way, (token,))
    other_shards = swapped(shards, "rep", 1)
    mine, sent, low_field, high_field = call(
        functools.partial(outer_kernel, side, rows, half),
        (
            like((spaces, padded, LANES), f32),
            like((spaces * padded + slots * area, LANES), bf16),
            edge_shape,
            edge_shape,
        ),
        "ssvvvva",
        [
            pltpu.VMEM((slots * area, 9 * channels), bf16),
            pltpu.VMEM((27 * channels + 16, channels), f32),
        ],
        flops // 5,
    )(counts, neighbors, acts, other_grads, far, sums, shards)
    received = swapped(sent, "rep", 1)
    def whole_filter(after):
        return call(
            filter_kernel,
            like((9 * channels, 3 * channels), bf16),
            "vva",
            [pltpu.VMEM((channels, 27 * channels), f32)],
            10**6,
        )(shards, other_shards, after)

    most = (slots + 3) // 4 * 2
    any_place, vector_place = (pl.BlockSpec(memory_space=place) for place in (pl.ANY, pltpu.VMEM))
    scratch = [pltpu.VMEM((voxels + 2 * area, 9 * channels), bf16)] * 2
    scratch += [pltpu.VMEM((voxels + 2 * area, 3 * channels), f32)]
    edge_buffer = pltpu.VMEM((2 * slots + 1,) + edge_shape.shape[1:], f32)
    token_shape = like((8, LANES), f32)

    def input_first(wide_filt, after):
        return call(
            functools.partial(input_first_kernel, side, spaces * padded),
            (like((most, voxels, channels), bf16), token_shape),
            "sssvvvvvva",
            [edge_buffer] * 2 + scratch,
            flops // 2,
        )(
            counts, neighbors, other_neighbors, field, low_field, high_field, near, received,
            wide_filt, after,
        )

    def input_rest(wide_filt, done, returned, after):
        return call(
            functools.partial(input_rest_kernel, side),
            (like(acts.shape, bf16), token_shape),
            "ssvvvvvva",
            [pltpu.VMEM((slots + 1, voxels, channels), bf16), pltpu.VMEM((voxels, channels), bf16)]
            + scratch
            + [pltpu.SemaphoreType.DMA((slots,))],
            flops // 2,
            out_specs=(any_place, vector_place),
        )(counts, neighbors, field, low_field, high_field, wide_filt, done, returned, after)

    held, arrived = mine, [received]
    passed, waits = [], []
    for number, (unit, members) in enumerate(steps):
        blocks = held.shape[0] // members
        inputs = [held, *arrived, *passed, *waits]
        outs = call(
            functools.partial(
                reduce_kernel, unit, members, len(arrived), len(passed), len(waits)
            ),
            (like((blocks, padded, LANES), f32),)
            + (like((blocks, padded, LANES), bf16),) * (members - 1)
            + tuple(like(x.shape, x.dtype) for x in passed),
            "v" * (1 + len(arrived)) + "a" * (len(passed) + len(waits)),
            [],
            10**6,
            out_specs=(vector_place,) * members + (any_place,) * len(passed),
            aliases={1 + len(arrived) + i: members + i for i in range(len(passed))},
        )(*inputs)
        held, sends, passed = outs[0], outs[1:members], outs[members:]
        arrived = [swapped(block, "space", unit * (m + 1)) for m, block in enumerate(sends)]
        if number == 0:
            wide_filt = whole_filter(sends[0])
            give, token = input_first(wide_filt, sends[0])
            passed, waits = [give], [token]
        if number == 1:
            returned = swapped(passed[0], "rep", 1)
            input_grad, token = input_rest(wide_filt, passed[0], returned, sends[0])
            passed, waits = [], [token]
    filt_grad = call(
        functools.partial(last_kernel, 1.0 / math.sqrt(slots * devices * voxels), half, len(arrived)),
        like(filt.shape[::-1], f32),
        "v" * (1 + len(arrived)) + "a" * len(waits),
        [],
        10**6,
    )(held, *arrived, *waits)
    return input_grad, filt_grad.T


def solution(mesh):
    in_specs = (
        P(AXES, None, None),
        P(AXES, None, None),
        P(AXES, None, None),
        P("space", "rep"),
        P(),
        P(AXES, None),
    )
    out_specs = (P(AXES, None, None), P("space", "rep"))
    return jax.shard_map(
        on_device, mesh=mesh, in_specs=in_specs, out_specs=out_specs, check_vma=False
    )
```

profile of v0, /device:TPU:0, one launch (start us, length us, event | category | flops | bytes accessed | tf_op | source)
XLA Modules:
  0.0 49.0 jit_solution(12692013686845428912)
XLA Ops:
  0.6 4.1 %collective-permute-start.1 = (bf16[1,64,216]{2,1,0:T(8,128)(2,1)}, bf16[1,64,216]{2,1,0:T(8,128)(2,1)S(1)}, u32[]{:S(2)}, u32[]{:S(2)}) collective-permute-start(bf16[1,64,216]{2,1,0:T(8,128)(2,1)} %bitcast.4), channel_id=1, source_target_pairs={{0,16},{2,18},{4,20},{6,22},{8,24},{10,26},{12,28},{14,30},{16,0},... | collective-permute-start | bytes 82952 | tf_op jit(solution)/shard_map/ppermute | solution.py:36
  4.7 2.7 %shard_map.77 = (bf16[12,512,128]{2,1,0:T(8,128)(2,1)S(1)}, bf16[12,64,128]{2,1,0:T(8,128)(2,1)S(1)}, bf16[12,64,128]{2,1,0:T(8,128)(2,1)S(1)}, bf16[12,512,128]{2,1,0:T(8,128)(2,1)S(1)}) custom-call(bf16[12,512,128]{2,1,0:T(8,128)(2,1)} %acts_far.1, bf16[12,512,128]{2,1,0:T(8,128)(2,1)} %preact_far.1, bf16[12,512,128]{2,1,0:T(8,128)(2,1)} %cotangent_far.1), custom_call_target="tpu_custom_call" | custom-call | flops 1087163648 | bytes 1048576 | tf_op jit(solution)/shard_map/pallas_call | solution.py:496
  8.1 1.6 %collective-permute-start.4 = (bf16[2,64,216]{2,1,0:T(8,128)(2,1)S(1)}, bf16[2,64,216]{2,1,0:T(8,128)(2,1)S(1)}, u32[]{:S(2)}, u32[]{:S(2)}) collective-permute-start(bf16[2,64,216]{2,1,0:T(8,128)(2,1)S(1)} %get-tuple-element.35.refs_0_), channel_id=1, source_target_pairs={{0,8},{2,10},{4,12},{6,14},{8,0},{10,2},{12,4},{14,6},{16,24},{18,... | collective-permute-start | bytes 165896 | tf_op jit(solution)/shard_map/ppermute | solution.py:36
  9.7 0.7 %collective-permute-start.5 = (bf16[12,64,128]{2,1,0:T(8,128)(2,1)S(1)}, bf16[12,64,128]{2,1,0:T(8,128)(2,1)S(1)}, u32[]{:S(2)}, u32[]{:S(2)}) collective-permute-start(bf16[12,64,128]{2,1,0:T(8,128)(2,1)S(1)} %get-tuple-element.37), channel_id=1, source_target_pairs={{1,2},{2,1},{3,4},{4,3},{5,6},{6,5},{7,8},{8,7},{9,10},{10,9},{11,... | collective-permute-start | bytes 589832 | tf_op jit(solution)/shard_map/ppermute | solution.py:31
  10.4 2.0 %collective-permute-done.4.refs_1_ = bf16[2,64,216]{2,1,0:T(8,128)(2,1)S(1)} collective-permute-done((bf16[2,64,216]{2,1,0:T(8,128)(2,1)S(1)}, bf16[2,64,216]{2,1,0:T(8,128)(2,1)S(1)}, u32[]{:S(2)}, u32[]{:S(2)}) %collective-permute-start.4) | collective-permute-done | bytes 55328 | tf_op jit(solution)/shard_map/ppermute | solution.py:36
  12.4 1.6 %collective-permute-start.6 = (bf16[4,64,216]{2,1,0:T(8,128)(2,1)S(1)}, bf16[4,64,216]{2,1,0:T(8,128)(2,1)S(1)}, u32[]{:S(2)}, u32[]{:S(2)}) collective-permute-start(bf16[4,64,216]{2,1,0:T(8,128)(2,1)S(1)} %shard_map.79.after.refs_0_), channel_id=1, source_target_pairs={{0,2},{2,0},{4,6},{6,4},{8,10},{10,8},{12,14},{14,12},{16,18},{18,... | collective-permute-start | bytes 331784 | tf_op jit(solution)/shard_map/ppermute | solution.py:36
  13.9 1.5 %collective-permute-start.7 = (bf16[4,64,216]{2,1,0:T(8,128)(2,1)S(1)}, bf16[4,64,216]{2,1,0:T(8,128)(2,1)S(1)}, u32[]{:S(2)}, u32[]{:S(2)}) collective-permute-start(bf16[4,64,216]{2,1,0:T(8,128)(2,1)S(1)} %shard_map.79.after.refs_0_), channel_id=1, source_target_pairs={{0,4},{2,6},{4,0},{6,2},{8,12},{10,14},{12,8},{14,10},{16,20},{18,... | collective-permute-start | bytes 331784 | tf_op jit(solution)/shard_map/ppermute | solution.py:36
  15.5 0.8 %collective-permute-start.8 = (bf16[4,64,216]{2,1,0:T(8,128)(2,1)S(1)}, bf16[4,64,216]{2,1,0:T(8,128)(2,1)S(1)}, u32[]{:S(2)}, u32[]{:S(2)}) collective-permute-start(bf16[4,64,216]{2,1,0:T(8,128)(2,1)S(1)} %shard_map.79.after.refs_0_), channel_id=1, source_target_pairs={{0,6},{2,4},{4,2},{6,0},{8,14},{10,12},{12,10},{14,8},{16,22},{18,... | collective-permute-start | bytes 331784 | tf_op jit(solution)/shard_map/ppermute | solution.py:36
  16.3 2.6 %shard_map.80 = (f32[384,1152]{1,0:T(8,128)S(1)}, f32[25,8,8,8,128]{4,3,2,1,0:T(8,128)S(1)}, f32[8,128]{1,0:T(8,128)S(1)}) custom-call(s32[32]{0:T(128)S(1)} %copy-done.2, s32[12,27]{1,0:T(8,128)S(1)} %copy-done.1, s32[12,27]{1,0:T(8,128)S(1)} %collective-permute-done.other_neighbors, bf16[12,512,128]{2,1,0:T(8,128)(2,1)S(1)} %get-tuple-element.33.acts, ...), custom_call_target="tpu_custom_call" | custom-call | flops 5435817984 | bytes 1048576 | tf_op jit(solution)/shard_map/pallas_call | solution.py:510
  18.9 3.1 %collective-permute-done.6.refs_1_ = bf16[4,64,216]{2,1,0:T(8,128)(2,1)S(1)} collective-permute-done((bf16[4,64,216]{2,1,0:T(8,128)(2,1)S(1)}, bf16[4,64,216]{2,1,0:T(8,128)(2,1)S(1)}, u32[]{:S(2)}, u32[]{:S(2)}) %collective-permute-start.6) | collective-permute-done | bytes 110624 | tf_op jit(solution)/shard_map/ppermute | solution.py:36
  22.0 1.9 %collective-permute-done.8.refs_3_ = bf16[4,64,216]{2,1,0:T(8,128)(2,1)S(1)} collective-permute-done((bf16[4,64,216]{2,1,0:T(8,128)(2,1)S(1)}, bf16[4,64,216]{2,1,0:T(8,128)(2,1)S(1)}, u32[]{:S(2)}, u32[]{:S(2)}) %collective-permute-start.8) | collective-permute-done | bytes 110624 | tf_op jit(solution)/shard_map/ppermute | solution.py:36
  24.0 2.4 %shard_map.82 = (f32[16,112,128]{2,1,0:T(8,128)S(1)}, bf16[2560,128]{1,0:T(8,128)(2,1)S(1)}, f32[13,1,8,8,128]{4,3,2,1,0:T(8,128)S(1)}, f32[13,1,8,8,128]{4,3,2,1,0:T(8,128)S(1)}) custom-call(s32[32]{0:T(128)S(1)} %copy-done.2, s32[12,27]{1,0:T(8,128)S(1)} %copy-done.1, bf16[12,512,128]{2,1,0:T(8,128)(2,1)S(1)} %get-tuple-element.33.acts, ...), custom_call_target="tpu_custom_call" | custom-call | flops 1087163648 | bytes 1048576 | tf_op jit(solution)/shard_map/pallas_call | solution.py:520
  27.0 1.6 %collective-permute-done.10.refs_0_.arrived = bf16[2560,128]{1,0:T(8,128)(2,1)S(1)} collective-permute-done((bf16[2560,128]{1,0:T(8,128)(2,1)S(1)}, bf16[2560,128]{1,0:T(8,128)(2,1)S(1)}, u32[]{:S(2)}, u32[]{:S(2)}) %collective-permute-start.10) | collective-permute-done | bytes 655392 | tf_op jit(solution)/shard_map/ppermute | solution.py:36
  28.6 3.0 %collective-permute-start.11 = (bf16[4,112,128]{2,1,0:T(8,128)(2,1)S(1)}, bf16[4,112,128]{2,1,0:T(8,128)(2,1)S(1)}, u32[]{:S(2)}, u32[]{:S(2)}) collective-permute-start(bf16[4,112,128]{2,1,0:T(8,128)(2,1)S(1)} %get-tuple-element.44.after), channel_id=1, source_target_pairs={{0,2},{2,0},{4,6},{6,4},{8,10},{10,8},{12,14},{14,12},{16,18},{18,... | collective-permute-start | bytes 344072 | tf_op jit(solution)/shard_map/ppermute | solution.py:36
  31.6 1.5 %collective-permute-start.13 = (bf16[4,112,128]{2,1,0:T(8,128)(2,1)S(1)}, bf16[4,112,128]{2,1,0:T(8,128)(2,1)S(1)}, u32[]{:S(2)}, u32[]{:S(2)}) collective-permute-start(bf16[4,112,128]{2,1,0:T(8,128)(2,1)S(1)} %get-tuple-element.47), channel_id=1, source_target_pairs={{0,6},{2,4},{4,2},{6,0},{8,14},{10,12},{12,10},{14,8},{16,22},{18,... | collective-permute-start | bytes 344072 | tf_op jit(solution)/shard_map/ppermute | solution.py:36
  33.2 0.5 %shard_map.84.filt = bf16[1152,384]{1,0:T(8,128)(2,1)S(1)} custom-call(bf16[16,64,216]{2,1,0:T(8,128)(2,1)S(1)} %shard_map.81.after.held, bf16[16,64,216]{2,1,0:T(8,128)(2,1)S(1)} %collective-permute-done.9.arrived, bf16[4,112,128]{2,1,0:T(8,128)(2,1)S(1)} %get-tuple-element.44.after), custom_call_target="tpu_custom_call" | custom-call | flops 1000000 | bytes 1048576 | tf_op jit(solution)/shard_map/pallas_call | solution.py:537
  33.7 3.0 %shard_map.85 = (bf16[6,512,128]{2,1,0:T(8,128)(2,1)S(1)}, f32[8,128]{1,0:T(8,128)S(1)}) custom-call(s32[32]{0:T(128)S(1)} %copy-done.2, s32[12,27]{1,0:T(8,128)S(1)} %copy-done.1, s32[12,27]{1,0:T(8,128)S(1)} %collective-permute-done.other_neighbors, f32[25,8,8,8,128]{4,3,2,1,0:T(8,128)S(1)} %get-tuple-element.36.field, ...), custom_call_target="tpu_custom_call" | custom-call | flops 2717908992 | bytes 1048576 | tf_op jit(solution)/shard_map/pallas_call | solution.py:553
  36.7 2.3 %collective-permute-done.12.refs_1_ = bf16[4,112,128]{2,1,0:T(8,128)(2,1)S(1)} collective-permute-done((bf16[4,112,128]{2,1,0:T(8,128)(2,1)S(1)}, bf16[4,112,128]{2,1,0:T(8,128)(2,1)S(1)}, u32[]{:S(2)}, u32[]{:S(2)}) %collective-permute-start.12) | collective-permute-done | bytes 114720 | tf_op jit(solution)/shard_map/ppermute | solution.py:36
  39.1 1.3 %collective-permute-start.15 = (bf16[1,112,128]{2,1,0:T(8,128)(2,1)S(1)}, bf16[1,112,128]{2,1,0:T(8,128)(2,1)S(1)}, u32[]{:S(2)}, u32[]{:S(2)}) collective-permute-start(bf16[1,112,128]{2,1,0:T(8,128)(2,1)S(1)} %get-tuple-element.52.after), channel_id=1, source_target_pairs={{0,8},{2,10},{4,12},{6,14},{8,0},{10,2},{12,4},{14,6},{16,24},{18,... | collective-permute-start | bytes 86024 | tf_op jit(solution)/shard_map/ppermute | solution.py:36
  40.4 2.1 %collective-permute-start.16 = (bf16[1,112,128]{2,1,0:T(8,128)(2,1)S(1)}, bf16[1,112,128]{2,1,0:T(8,128)(2,1)S(1)}, u32[]{:S(2)}, u32[]{:S(2)}) collective-permute-start(bf16[1,112,128]{2,1,0:T(8,128)(2,1)S(1)} %get-tuple-element.55), channel_id=1, source_target_pairs={{0,16},{2,18},{4,20},{6,22},{8,24},{10,26},{12,28},{14,30},{16,0},... | collective-permute-start | bytes 86024 | tf_op jit(solution)/shard_map/ppermute | solution.py:36
  42.5 1.4 %collective-permute-start.17 = (bf16[1,112,128]{2,1,0:T(8,128)(2,1)S(1)}, bf16[1,112,128]{2,1,0:T(8,128)(2,1)S(1)}, u32[]{:S(2)}, u32[]{:S(2)}) collective-permute-start(bf16[1,112,128]{2,1,0:T(8,128)(2,1)S(1)} %get-tuple-element.56), channel_id=1, source_target_pairs={{0,24},{2,26},{4,28},{6,30},{8,16},{10,18},{12,20},{14,22},{16,8},... | collective-permute-start | bytes 86024 | tf_op jit(solution)/shard_map/ppermute | solution.py:36
  43.9 1.9 %shard_map.87 = (bf16[12,512,128]{2,1,0:T(8,128)(2,1)}, f32[8,128]{1,0:T(8,128)S(1)}) custom-call(s32[32]{0:T(128)S(1)} %copy-done.2, s32[12,27]{1,0:T(8,128)S(1)} %copy-done.1, f32[25,8,8,8,128]{4,3,2,1,0:T(8,128)S(1)} %get-tuple-element.36.field, f32[13,1,8,8,128]{4,3,2,1,0:T(8,128)S(1)} %get-tuple-element.40.low, ...), custom_call_target="tpu_custom_call" | custom-call | flops 2717908992 | bytes 1048576 | tf_op jit(solution)/shard_map/pallas_call | solution.py:565
  45.9 2.3 %collective-permute-done.17.refs_2_ = bf16[1,112,128]{2,1,0:T(8,128)(2,1)S(1)} collective-permute-done((bf16[1,112,128]{2,1,0:T(8,128)(2,1)S(1)}, bf16[1,112,128]{2,1,0:T(8,128)(2,1)S(1)}, u32[]{:S(2)}, u32[]{:S(2)}) %collective-permute-start.17) | collective-permute-done | bytes 28704 | tf_op jit(solution)/shard_map/ppermute | solution.py:36
  48.2 0.8 %shard_map.88 = f32[64,216]{1,0:T(8,128)} custom-call(f32[1,112,128]{2,1,0:T(8,128)S(1)} %get-tuple-element.54.held, bf16[1,112,128]{2,1,0:T(8,128)(2,1)S(1)} %collective-permute-done.15.refs_0_, bf16[1,112,128]{2,1,0:T(8,128)(2,1)S(1)} %collective-permute-done.16.refs_1_, bf16[1,112,128]{2,1,0:T(8,128)(2,1)S(1)} %collective-permute-done.17.refs_2_, ...), custom_call_target="tpu_custom_call" | custom-call | flops 1000000 | bytes 1048576 | tf_op jit(solution)/shard_map/pallas_call | solution.py:604
  (30 shorter events, 1.5 us)
Async XLA Ops:
  0.6 6.9 %copy-start = (bf16[216,64]{0,1:T(8,128)(2,1)S(1)}, bf16[216,64]{0,1:T(8,128)(2,1)}, u32[]{:S(2)}) copy-start(bf16[216,64]{0,1:T(8,128)(2,1)} %param.9) | copy-start | bytes 82948
  0.6 6.8 %collective-permute-start.1 = (bf16[1,64,216]{2,1,0:T(8,128)(2,1)}, bf16[1,64,216]{2,1,0:T(8,128)(2,1)S(1)}, u32[]{:S(2)}, u32[]{:S(2)}) collective-permute-start(bf16[1,64,216]{2,1,0:T(8,128)(2,1)} %bitcast.4), channel_id=1, source_target_pairs={{0,16},{2,18},{4,20},{6,22},{8,24},{10,26},{12,28},{14,30},{16,0},... | collective-permute-start | bytes 82952 | tf_op jit(solution)/shard_map/ppermute | solution.py:36
  7.5 2.2 %copy-start.1 = (s32[12,27]{1,0:T(8,128)S(1)}, s32[12,27]{1,0:T(8,128)}, u32[]{:S(2)}) copy-start(s32[12,27]{1,0:T(8,128)} %neighbors.7) | copy-start | bytes 3892
  7.5 8.8 %copy-start.2 = (s32[32]{0:T(128)S(1)}, s32[32]{0:T(128)}, u32[]{:S(2)}) copy-start(s32[32]{0:T(128)} %counts.7) | copy-start | bytes 388
  7.5 7.9 %collective-permute-start.2 = (bf16[12,512,128]{2,1,0:T(8,128)(2,1)S(1)}, bf16[12,512,128]{2,1,0:T(8,128)(2,1)S(1)}, u32[]{:S(2)}, u32[]{:S(2)}) collective-permute-start(bf16[12,512,128]{2,1,0:T(8,128)(2,1)S(1)} %get-tuple-element.33.acts), channel_id=1, source_target_pairs={{0,1},{1,0},{2,3},{3,2},{4,5},{5,4},{6,7},{7,6},{8,9},{9,8},{10,11... | collective-permute-start | bytes 4718600 | tf_op jit(solution)/shard_map/ppermute | solution.py:36
  7.6 8.7 %collective-permute-start.3 = (bf16[12,512,128]{2,1,0:T(8,128)(2,1)S(1)}, bf16[12,512,128]{2,1,0:T(8,128)(2,1)S(1)}, u32[]{:S(2)}, u32[]{:S(2)}) collective-permute-start(bf16[12,512,128]{2,1,0:T(8,128)(2,1)S(1)} %get-tuple-element.34.grads), channel_id=1, source_target_pairs={{0,1},{1,0},{2,3},{3,2},{4,5},{5,4},{6,7},{7,6},{8,9},{9,8},{10,11... | collective-permute-start | bytes 4718600 | tf_op jit(solution)/shard_map/ppermute | solution.py:36
  8.1 4.3 %collective-permute-start.4 = (bf16[2,64,216]{2,1,0:T(8,128)(2,1)S(1)}, bf16[2,64,216]{2,1,0:T(8,128)(2,1)S(1)}, u32[]{:S(2)}, u32[]{:S(2)}) collective-permute-start(bf16[2,64,216]{2,1,0:T(8,128)(2,1)S(1)} %get-tuple-element.35.refs_0_), channel_id=1, source_target_pairs={{0,8},{2,10},{4,12},{6,14},{8,0},{10,2},{12,4},{14,6},{16,24},{18,... | collective-permute-start | bytes 165896 | tf_op jit(solution)/shard_map/ppermute | solution.py:36
  9.7 4.3 %collective-permute-start = (s32[12,27]{1,0:T(8,128)S(1)}, s32[12,27]{1,0:T(8,128)S(1)}, u32[]{:S(2)}, u32[]{:S(2)}) collective-permute-start(s32[12,27]{1,0:T(8,128)S(1)} %copy-done.1), channel_id=1, source_target_pairs={{0,1},{1,0},{2,3},{3,2},{4,5},{5,4},{6,7},{7,6},{8,9},{9,8},{10,11... | collective-permute-start | bytes 3896 | tf_op jit(solution)/shard_map/ppermute | solution.py:36
  9.7 14.3 %collective-permute-start.5 = (bf16[12,64,128]{2,1,0:T(8,128)(2,1)S(1)}, bf16[12,64,128]{2,1,0:T(8,128)(2,1)S(1)}, u32[]{:S(2)}, u32[]{:S(2)}) collective-permute-start(bf16[12,64,128]{2,1,0:T(8,128)(2,1)S(1)} %get-tuple-element.37), channel_id=1, source_target_pairs={{1,2},{2,1},{3,4},{4,3},{5,6},{6,5},{7,8},{8,7},{9,10},{10,9},{11,... | collective-permute-start | bytes 589832 | tf_op jit(solution)/shard_map/ppermute | solution.py:31
  12.4 9.6 %collective-permute-start.6 = (bf16[4,64,216]{2,1,0:T(8,128)(2,1)S(1)}, bf16[4,64,216]{2,1,0:T(8,128)(2,1)S(1)}, u32[]{:S(2)}, u32[]{:S(2)}) collective-permute-start(bf16[4,64,216]{2,1,0:T(8,128)(2,1)S(1)} %shard_map.79.after.refs_0_), channel_id=1, source_target_pairs={{0,2},{2,0},{4,6},{6,4},{8,10},{10,8},{12,14},{14,12},{16,18},{18,... | collective-permute-start | bytes 331784 | tf_op jit(solution)/shard_map/ppermute | solution.py:36
  13.9 8.1 %collective-permute-start.7 = (bf16[4,64,216]{2,1,0:T(8,128)(2,1)S(1)}, bf16[4,64,216]{2,1,0:T(8,128)(2,1)S(1)}, u32[]{:S(2)}, u32[]{:S(2)}) collective-permute-start(bf16[4,64,216]{2,1,0:T(8,128)(2,1)S(1)} %shard_map.79.after.refs_0_), channel_id=1, source_target_pairs={{0,4},{2,6},{4,0},{6,2},{8,12},{10,14},{12,8},{14,10},{16,20},{18,... | collective-permute-start | bytes 331784 | tf_op jit(solution)/shard_map/ppermute | solution.py:36
  15.5 8.5 %collective-permute-start.8 = (bf16[4,64,216]{2,1,0:T(8,128)(2,1)S(1)}, bf16[4,64,216]{2,1,0:T(8,128)(2,1)S(1)}, u32[]{:S(2)}, u32[]{:S(2)}) collective-permute-start(bf16[4,64,216]{2,1,0:T(8,128)(2,1)S(1)} %shard_map.79.after.refs_0_), channel_id=1, source_target_pairs={{0,6},{2,4},{4,2},{6,0},{8,14},{10,12},{12,10},{14,8},{16,22},{18,... | collective-permute-start | bytes 331784 | tf_op jit(solution)/shard_map/ppermute | solution.py:36
  26.4 2.2 %collective-permute-start.10 = (bf16[2560,128]{1,0:T(8,128)(2,1)S(1)}, bf16[2560,128]{1,0:T(8,128)(2,1)S(1)}, u32[]{:S(2)}, u32[]{:S(2)}) collective-permute-start(bf16[2560,128]{1,0:T(8,128)(2,1)S(1)} %get-tuple-element.43), channel_id=1, source_target_pairs={{0,1},{1,0},{2,3},{3,2},{4,5},{5,4},{6,7},{7,6},{8,9},{9,8},{10,11... | collective-permute-start | bytes 1966088 | tf_op jit(solution)/shard_map/ppermute | solution.py:36
  26.5 6.7 %collective-permute-start.9 = (bf16[16,64,216]{2,1,0:T(8,128)(2,1)S(1)}, bf16[16,64,216]{2,1,0:T(8,128)(2,1)S(1)}, u32[]{:S(2)}, u32[]{:S(2)}) collective-permute-start(bf16[16,64,216]{2,1,0:T(8,128)(2,1)S(1)} %shard_map.81.after.held), channel_id=1, source_target_pairs={{0,1},{1,0},{2,3},{3,2},{4,5},{5,4},{6,7},{7,6},{8,9},{9,8},{10,11... | collective-permute-start | bytes 1327112 | tf_op jit(solution)/shard_map/ppermute | solution.py:36
  28.6 8.0 %collective-permute-start.11 = (bf16[4,112,128]{2,1,0:T(8,128)(2,1)S(1)}, bf16[4,112,128]{2,1,0:T(8,128)(2,1)S(1)}, u32[]{:S(2)}, u32[]{:S(2)}) collective-permute-start(bf16[4,112,128]{2,1,0:T(8,128)(2,1)S(1)} %get-tuple-element.44.after), channel_id=1, source_target_pairs={{0,2},{2,0},{4,6},{6,4},{8,10},{10,8},{12,14},{14,12},{16,18},{18,... | collective-permute-start | bytes 344072 | tf_op jit(solution)/shard_map/ppermute | solution.py:36
  31.6 7.4 %collective-permute-start.12 = (bf16[4,112,128]{2,1,0:T(8,128)(2,1)S(1)}, bf16[4,112,128]{2,1,0:T(8,128)(2,1)S(1)}, u32[]{:S(2)}, u32[]{:S(2)}) collective-permute-start(bf16[4,112,128]{2,1,0:T(8,128)(2,1)S(1)} %get-tuple-element.46), channel_id=1, source_target_pairs={{0,4},{2,6},{4,0},{6,2},{8,12},{10,14},{12,8},{14,10},{16,20},{18,... | collective-permute-start | bytes 344072 | tf_op jit(solution)/shard_map/ppermute | solution.py:36
  31.6 7.4 %collective-permute-start.13 = (bf16[4,112,128]{2,1,0:T(8,128)(2,1)S(1)}, bf16[4,112,128]{2,1,0:T(8,128)(2,1)S(1)}, u32[]{:S(2)}, u32[]{:S(2)}) collective-permute-start(bf16[4,112,128]{2,1,0:T(8,128)(2,1)S(1)} %get-tuple-element.47), channel_id=1, source_target_pairs={{0,6},{2,4},{4,2},{6,0},{8,14},{10,12},{12,10},{14,8},{16,22},{18,... | collective-permute-start | bytes 344072 | tf_op jit(solution)/shard_map/ppermute | solution.py:36
  39.1 4.9 %collective-permute-start.14 = (bf16[6,512,128]{2,1,0:T(8,128)(2,1)S(1)}, bf16[6,512,128]{2,1,0:T(8,128)(2,1)S(1)}, u32[]{:S(2)}, u32[]{:S(2)}) collective-permute-start(bf16[6,512,128]{2,1,0:T(8,128)(2,1)S(1)} %get-tuple-element.51.done), channel_id=1, source_target_pairs={{0,1},{1,0},{2,3},{3,2},{4,5},{5,4},{6,7},{7,6},{8,9},{9,8},{10,11... | collective-permute-start | bytes 2359304 | tf_op jit(solution)/shard_map/ppermute | solution.py:36
  39.1 6.7 %collective-permute-start.15 = (bf16[1,112,128]{2,1,0:T(8,128)(2,1)S(1)}, bf16[1,112,128]{2,1,0:T(8,128)(2,1)S(1)}, u32[]{:S(2)}, u32[]{:S(2)}) collective-permute-start(bf16[1,112,128]{2,1,0:T(8,128)(2,1)S(1)} %get-tuple-element.52.after), channel_id=1, source_target_pairs={{0,8},{2,10},{4,12},{6,14},{8,0},{10,2},{12,4},{14,6},{16,24},{18,... | collective-permute-start | bytes 86024 | tf_op jit(solution)/shard_map/ppermute | solution.py:36
  40.4 5.5 %collective-permute-start.16 = (bf16[1,112,128]{2,1,0:T(8,128)(2,1)S(1)}, bf16[1,112,128]{2,1,0:T(8,128)(2,1)S(1)}, u32[]{:S(2)}, u32[]{:S(2)}) collective-permute-start(bf16[1,112,128]{2,1,0:T(8,128)(2,1)S(1)} %get-tuple-element.55), channel_id=1, source_target_pairs={{0,16},{2,18},{4,20},{6,22},{8,24},{10,26},{12,28},{14,30},{16,0},... | collective-permute-start | bytes 86024 | tf_op jit(solution)/shard_map/ppermute | solution.py:36
  42.5 5.7 %collective-permute-start.17 = (bf16[1,112,128]{2,1,0:T(8,128)(2,1)S(1)}, bf16[1,112,128]{2,1,0:T(8,128)(2,1)S(1)}, u32[]{:S(2)}, u32[]{:S(2)}) collective-permute-start(bf16[1,112,128]{2,1,0:T(8,128)(2,1)S(1)} %get-tuple-element.56), channel_id=1, source_target_pairs={{0,24},{2,26},{4,28},{6,30},{8,16},{10,18},{12,20},{14,22},{16,8},... | collective-permute-start | bytes 86024 | tf_op jit(solution)/shard_map/ppermute | solution.py:36
where the time goes:
time: 49.2 us; the launch traced here: 49 us
  starting transfers between devices  20.7 us (42%)
  Pallas kernels  14.1 us (29%)
  waiting for transfers between devices  13.3 us (27%)
  between operations  0.81 us (2%)
    ppermute x17, starting transfers between devices, swapped(): return lax.ppermute(x, axis, [(i, i ^ mask) for i in range(count)])  20.1 us
    ppermute x17, waiting for transfers between devices, swapped(): return lax.ppermute(x, axis, [(i, i ^ mask) for i in range(count)])  13.3 us
    pallas_call x1, Pallas kernels, input_first(): call(functools.partial(input_first_kernel, side, spaces * padded), (like(...  3.01 us
    pallas_call x1, Pallas kernels, on_device(): call(functools.partial(gate_kernel, side), (like(acts.shape, bf16), plane...  2.72 us
    pallas_call x1, Pallas kernels, on_device(): call(functools.partial(inner_kernel, side), (sums_shape, field_shape, lik...  2.57 us
    pallas_call x1, Pallas kernels, on_device(): call(functools.partial(outer_kernel, side, rows, half), (like((spaces, pa...  2.4 us
    pallas_call x1, Pallas kernels, input_rest(): call(functools.partial(input_rest_kernel, side), (like(acts.shape, bf16),...  1.93 us
  transfers between devices with their start and end apart: 18, of which 6 were waited for; matrix products, arithmetic and copies ran while one was open for 0% of the time, Pallas kernels for 22%

commit v1 on v0

--- a/solution.py
+++ b/solution.py
@@ -215,7 +215,7 @@
 
 def outer_kernel(
     side, rows, half, counts, neighbors, acts, other_grads, far, sums, after,
-    mine, sent, low_field, high_field, unrolled, table_sum,
+    mine, sent, low_field, high_field, low_rows, high_rows, table_sum,
 ):
     position = lax.axis_index(AXES)
     rep = lax.axis_index("rep")
@@ -224,7 +224,10 @@
     area = side * side
     live = counts[position]
     extra = []
-    for layer, field, plane in ((0, low_field, 0), (2, high_field, side - 1)):
+    for layer, field, plane, unrolled in (
+        (0, low_field, 0, low_rows),
+        (2, high_field, side - 1, high_rows),
+    ):
         start = (side - 1) * area if layer == 0 else 0
         edge = jnp.where(rep == layer // 2, far[...], other_grads[:, start : start + area])
         field[0:slots] = edge.astype(f32).reshape(field[0:slots].shape)
@@ -329,9 +332,13 @@
         fill(unrolled[turn], (side + 1) * area, high, 0, table_of(brick, 2), side)
 
     def finish(brick, turn):
-        product[...] = jnp.dot(unrolled[turn][...], filt[...], preferred_element_type=f32)
-        values = product[2 * area :, 0:LANES] + product[area : area + voxels, LANES : 2 * LANES]
-        values = values + product[0:voxels, 2 * LANES :]
+        rows = unrolled[turn]
+        product[...] = jnp.dot(
+            rows[area:], filt[:, : 2 * LANES], preferred_element_type=f32
+        )
+        values = jnp.dot(rows[:voxels], filt[:, 2 * LANES :], preferred_element_type=f32)
+        values = values + product[area:, :LANES]
+        values = values + product[:voxels, LANES:]
         staged[brick - first] = values.astype(bf16)
 
     @pl.when(last > first)
@@ -528,6 +535,7 @@
         "ssvvvva",
         [
             pltpu.VMEM((slots * area, 9 * channels), bf16),
+            pltpu.VMEM((slots * area, 9 * channels), bf16),
             pltpu.VMEM((27 * channels + 16, channels), f32),
         ],
         flops // 5,
@@ -545,7 +553,7 @@
     most = (slots + 3) // 4 * 2
     any_place, vector_place = (pl.BlockSpec(memory_space=place) for place in (pl.ANY, pltpu.VMEM))
     scratch = [pltpu.VMEM((voxels + 2 * area, 9 * channels), bf16)] * 2
-    scratch += [pltpu.VMEM((voxels + 2 * area, 3 * channels), f32)]
+    scratch += [pltpu.VMEM((voxels + area, 2 * channels), f32)]
     edge_buffer = pltpu.VMEM((2 * slots + 1,) + edge_shape.shape[1:], f32)
     token_shape = like((8, LANES), f32)
 

time: 49.2 us -> 49.4 us (level)
  Pallas kernels: 14.1 us -> 22.7 us
  waiting for transfers between devices: 13.3 us -> 5.39 us
    ppermute x17, waiting for transfers between devices: 13.3 us -> 5.39 us  [swapped(): return lax.ppermute(x, axis, [(i, i ^ mask) for i in range(count)])]
    pallas_call x1, Pallas kernels: 2.57 us -> 6.73 us  [on_device(): call(functools.partial(inner_kernel, side), (sums_shape, field_shape, lik...]
    pallas_call x1, Pallas kernels: 1.93 us -> 5.05 us  [input_rest(): call(functools.partial(input_rest_kernel, side), (like(acts.shape, bf16),...]
    pallas_call x1, Pallas kernels: 3.01 us -> 4.41 us  [input_first(): call(functools.partial(input_first_kernel, side, spaces * padded), (like(...]
  transfers between devices with their start and end apart: 18 -> 18, of which waited for: 6 -> 4; matrix products, arithmetic and copies ran while one was open for 0% -> 0% of each run, Pallas kernels for 22% -> 40%
where the time goes in v1:
time: 49.4 us; the launch traced here: 49.3 us
  Pallas kernels  22.7 us (46%)
  starting transfers between devices  20.4 us (41%)
  waiting for transfers between devices  5.39 us (11%)
  between operations  0.83 us (2%)
    ppermute x17, starting transfers between devices, swapped(): return lax.ppermute(x, axis, [(i, i ^ mask) for i in range(count)])  19.8 us
    pallas_call x1, Pallas kernels, on_device(): call(functools.partial(inner_kernel, side), (sums_shape, field_shape, lik...  6.73 us
    ppermute x17, waiting for transfers between devices, swapped(): return lax.ppermute(x, axis, [(i, i ^ mask) for i in range(count)])  5.39 us
    pallas_call x1, Pallas kernels, input_rest(): call(functools.partial(input_rest_kernel, side), (like(acts.shape, bf16),...  5.05 us
    pallas_call x1, Pallas kernels, input_first(): call(functools.partial(input_first_kernel, side, spaces * padded), (like(...  4.41 us
    pallas_call x1, Pallas kernels, on_device(): call(functools.partial(gate_kernel, side), (like(acts.shape, bf16), plane...  2.72 us
    pallas_call x1, Pallas kernels, on_device(): call(functools.partial(outer_kernel, side, rows, half), (like((spaces, pa...  2.23 us
  transfers between devices with their start and end apart: 18, of which 4 were waited for; matrix products, arithmetic and copies ran while one was open for 0% of the time, Pallas kernels for 40%

profile of v1, /device:TPU:0, one launch (start us, length us, event | category | flops | bytes accessed | tf_op | source)
XLA Modules:
  0.0 49.3 jit_solution(10955092642688693373)
XLA Ops:
  0.6 4.1 %collective-permute-start.1 = (bf16[1,64,216]{2,1,0:T(8,128)(2,1)}, bf16[1,64,216]{2,1,0:T(8,128)(2,1)S(1)}, u32[]{:S(2)}, u32[]{:S(2)}) collective-permute-start(bf16[1,64,216]{2,1,0:T(8,128)(2,1)} %bitcast.4), channel_id=1, source_target_pairs={{0,16},{2,18},{4,20},{6,22},{8,24},{10,26},{12,28},{14,30},{16,0},... | collective-permute-start | bytes 82952 | tf_op jit(solution)/shard_map/ppermute | solution.py:36
  4.7 2.7 %shard_map.77 = (bf16[12,512,128]{2,1,0:T(8,128)(2,1)S(1)}, bf16[12,64,128]{2,1,0:T(8,128)(2,1)S(1)}, bf16[12,64,128]{2,1,0:T(8,128)(2,1)S(1)}, bf16[12,512,128]{2,1,0:T(8,128)(2,1)S(1)}) custom-call(bf16[12,512,128]{2,1,0:T(8,128)(2,1)} %acts_far.1, bf16[12,512,128]{2,1,0:T(8,128)(2,1)} %preact_far.1, bf16[12,512,128]{2,1,0:T(8,128)(2,1)} %cotangent_far.1), custom_call_target="tpu_custom_call" | custom-call | flops 1087163648 | bytes 1048576 | tf_op jit(solution)/shard_map/pallas_call | solution.py:503
  7.6 0.5 %collective-permute-start.3 = (bf16[12,512,128]{2,1,0:T(8,128)(2,1)S(1)}, bf16[12,512,128]{2,1,0:T(8,128)(2,1)S(1)}, u32[]{:S(2)}, u32[]{:S(2)}) collective-permute-start(bf16[12,512,128]{2,1,0:T(8,128)(2,1)S(1)} %get-tuple-element.34.grads), channel_id=1, source_target_pairs={{0,1},{1,0},{2,3},{3,2},{4,5},{5,4},{6,7},{7,6},{8,9},{9,8},{10,11... | collective-permute-start | bytes 4718600 | tf_op jit(solution)/shard_map/ppermute | solution.py:36
  8.1 1.6 %collective-permute-start.4 = (bf16[2,64,216]{2,1,0:T(8,128)(2,1)S(1)}, bf16[2,64,216]{2,1,0:T(8,128)(2,1)S(1)}, u32[]{:S(2)}, u32[]{:S(2)}) collective-permute-start(bf16[2,64,216]{2,1,0:T(8,128)(2,1)S(1)} %get-tuple-element.35.refs_0_), channel_id=1, source_target_pairs={{0,8},{2,10},{4,12},{6,14},{8,0},{10,2},{12,4},{14,6},{16,24},{18,... | collective-permute-start | bytes 165896 | tf_op jit(solution)/shard_map/ppermute | solution.py:36
  9.7 0.7 %collective-permute-start.5 = (bf16[12,64,128]{2,1,0:T(8,128)(2,1)S(1)}, bf16[12,64,128]{2,1,0:T(8,128)(2,1)S(1)}, u32[]{:S(2)}, u32[]{:S(2)}) collective-permute-start(bf16[12,64,128]{2,1,0:T(8,128)(2,1)S(1)} %get-tuple-element.37), channel_id=1, source_target_pairs={{1,2},{2,1},{3,4},{4,3},{5,6},{6,5},{7,8},{8,7},{9,10},{10,9},{11,... | collective-permute-start | bytes 589832 | tf_op jit(solution)/shard_map/ppermute | solution.py:31
  10.4 2.0 %collective-permute-done.4.refs_1_ = bf16[2,64,216]{2,1,0:T(8,128)(2,1)S(1)} collective-permute-done((bf16[2,64,216]{2,1,0:T(8,128)(2,1)S(1)}, bf16[2,64,216]{2,1,0:T(8,128)(2,1)S(1)}, u32[]{:S(2)}, u32[]{:S(2)}) %collective-permute-start.4) | collective-permute-done | bytes 55328 | tf_op jit(solution)/shard_map/ppermute | solution.py:36
  12.4 1.6 %collective-permute-start.6 = (bf16[4,64,216]{2,1,0:T(8,128)(2,1)S(1)}, bf16[4,64,216]{2,1,0:T(8,128)(2,1)S(1)}, u32[]{:S(2)}, u32[]{:S(2)}) collective-permute-start(bf16[4,64,216]{2,1,0:T(8,128)(2,1)S(1)} %shard_map.79.after.refs_0_), channel_id=1, source_target_pairs={{0,2},{2,0},{4,6},{6,4},{8,10},{10,8},{12,14},{14,12},{16,18},{18,... | collective-permute-start | bytes 331784 | tf_op jit(solution)/shard_map/ppermute | solution.py:36
  13.9 1.5 %collective-permute-start.7 = (bf16[4,64,216]{2,1,0:T(8,128)(2,1)S(1)}, bf16[4,64,216]{2,1,0:T(8,128)(2,1)S(1)}, u32[]{:S(2)}, u32[]{:S(2)}) collective-permute-start(bf16[4,64,216]{2,1,0:T(8,128)(2,1)S(1)} %shard_map.79.after.refs_0_), channel_id=1, source_target_pairs={{0,4},{2,6},{4,0},{6,2},{8,12},{10,14},{12,8},{14,10},{16,20},{18,... | collective-permute-start | bytes 331784 | tf_op jit(solution)/shard_map/ppermute | solution.py:36
  15.5 0.8 %collective-permute-start.8 = (bf16[4,64,216]{2,1,0:T(8,128)(2,1)S(1)}, bf16[4,64,216]{2,1,0:T(8,128)(2,1)S(1)}, u32[]{:S(2)}, u32[]{:S(2)}) collective-permute-start(bf16[4,64,216]{2,1,0:T(8,128)(2,1)S(1)} %shard_map.79.after.refs_0_), channel_id=1, source_target_pairs={{0,6},{2,4},{4,2},{6,0},{8,14},{10,12},{12,10},{14,8},{16,22},{18,... | collective-permute-start | bytes 331784 | tf_op jit(solution)/shard_map/ppermute | solution.py:36
  16.3 6.7 %shard_map.80 = (f32[384,1152]{1,0:T(8,128)S(1)}, f32[25,8,8,8,128]{4,3,2,1,0:T(8,128)S(1)}, f32[8,128]{1,0:T(8,128)S(1)}) custom-call(s32[32]{0:T(128)S(1)} %copy-done.2, s32[12,27]{1,0:T(8,128)S(1)} %copy-done.1, s32[12,27]{1,0:T(8,128)S(1)} %collective-permute-done.other_neighbors, bf16[12,512,128]{2,1,0:T(8,128)(2,1)S(1)} %get-tuple-element.33.acts, ...), custom_call_target="tpu_custom_call" | custom-call | flops 5435817984 | bytes 1048576 | tf_op jit(solution)/shard_map/pallas_call | solution.py:517
  23.1 0.9 %collective-permute-done.8.refs_3_ = bf16[4,64,216]{2,1,0:T(8,128)(2,1)S(1)} collective-permute-done((bf16[4,64,216]{2,1,0:T(8,128)(2,1)S(1)}, bf16[4,64,216]{2,1,0:T(8,128)(2,1)S(1)}, u32[]{:S(2)}, u32[]{:S(2)}) %collective-permute-start.8) | collective-permute-done | bytes 110624 | tf_op jit(solution)/shard_map/ppermute | solution.py:36
  24.0 2.2 %shard_map.82 = (f32[16,112,128]{2,1,0:T(8,128)S(1)}, bf16[2560,128]{1,0:T(8,128)(2,1)S(1)}, f32[13,1,8,8,128]{4,3,2,1,0:T(8,128)S(1)}, f32[13,1,8,8,128]{4,3,2,1,0:T(8,128)S(1)}) custom-call(s32[32]{0:T(128)S(1)} %copy-done.2, s32[12,27]{1,0:T(8,128)S(1)} %copy-done.1, bf16[12,512,128]{2,1,0:T(8,128)(2,1)S(1)} %get-tuple-element.33.acts, ...), custom_call_target="tpu_custom_call" | custom-call | flops 1087163648 | bytes 1048576 | tf_op jit(solution)/shard_map/pallas_call | solution.py:527
  26.3 0.5 %collective-permute-start.9 = (bf16[16,64,216]{2,1,0:T(8,128)(2,1)S(1)}, bf16[16,64,216]{2,1,0:T(8,128)(2,1)S(1)}, u32[]{:S(2)}, u32[]{:S(2)}) collective-permute-start(bf16[16,64,216]{2,1,0:T(8,128)(2,1)S(1)} %shard_map.81.after.held), channel_id=1, source_target_pairs={{0,1},{1,0},{2,3},{3,2},{4,5},{5,4},{6,7},{7,6},{8,9},{9,8},{10,11... | collective-permute-start | bytes 1327112 | tf_op jit(solution)/shard_map/ppermute | solution.py:36
  26.8 1.6 %collective-permute-done.10.refs_0_.arrived = bf16[2560,128]{1,0:T(8,128)(2,1)S(1)} collective-permute-done((bf16[2560,128]{1,0:T(8,128)(2,1)S(1)}, bf16[2560,128]{1,0:T(8,128)(2,1)S(1)}, u32[]{:S(2)}, u32[]{:S(2)}) %collective-permute-start.10) | collective-permute-done | bytes 655392 | tf_op jit(solution)/shard_map/ppermute | solution.py:36
  28.5 3.0 %collective-permute-start.11 = (bf16[4,112,128]{2,1,0:T(8,128)(2,1)S(1)}, bf16[4,112,128]{2,1,0:T(8,128)(2,1)S(1)}, u32[]{:S(2)}, u32[]{:S(2)}) collective-permute-start(bf16[4,112,128]{2,1,0:T(8,128)(2,1)S(1)} %get-tuple-element.44.after), channel_id=1, source_target_pairs={{0,2},{2,0},{4,6},{6,4},{8,10},{10,8},{12,14},{14,12},{16,18},{18,... | collective-permute-start | bytes 344072 | tf_op jit(solution)/shard_map/ppermute | solution.py:36
  31.5 1.5 %collective-permute-start.13 = (bf16[4,112,128]{2,1,0:T(8,128)(2,1)S(1)}, bf16[4,112,128]{2,1,0:T(8,128)(2,1)S(1)}, u32[]{:S(2)}, u32[]{:S(2)}) collective-permute-start(bf16[4,112,128]{2,1,0:T(8,128)(2,1)S(1)} %get-tuple-element.47), channel_id=1, source_target_pairs={{0,6},{2,4},{4,2},{6,0},{8,14},{10,12},{12,10},{14,8},{16,22},{18,... | collective-permute-start | bytes 344072 | tf_op jit(solution)/shard_map/ppermute | solution.py:36
  33.0 0.5 %shard_map.84.filt = bf16[1152,384]{1,0:T(8,128)(2,1)S(1)} custom-call(bf16[16,64,216]{2,1,0:T(8,128)(2,1)S(1)} %shard_map.81.after.held, bf16[16,64,216]{2,1,0:T(8,128)(2,1)S(1)} %collective-permute-done.9.arrived, bf16[4,112,128]{2,1,0:T(8,128)(2,1)S(1)} %get-tuple-element.44.after), custom_call_target="tpu_custom_call" | custom-call | flops 1000000 | bytes 1048576 | tf_op jit(solution)/shard_map/pallas_call | solution.py:545
  33.5 4.4 %shard_map.85 = (bf16[6,512,128]{2,1,0:T(8,128)(2,1)S(1)}, f32[8,128]{1,0:T(8,128)S(1)}) custom-call(s32[32]{0:T(128)S(1)} %copy-done.2, s32[12,27]{1,0:T(8,128)S(1)} %copy-done.1, s32[12,27]{1,0:T(8,128)S(1)} %collective-permute-done.other_neighbors, f32[25,8,8,8,128]{4,3,2,1,0:T(8,128)S(1)} %get-tuple-element.36.field, ...), custom_call_target="tpu_custom_call" | custom-call | flops 2717908992 | bytes 1048576 | tf_op jit(solution)/shard_map/pallas_call | solution.py:561
  37.9 0.9 %collective-permute-done.12.refs_1_ = bf16[4,112,128]{2,1,0:T(8,128)(2,1)S(1)} collective-permute-done((bf16[4,112,128]{2,1,0:T(8,128)(2,1)S(1)}, bf16[4,112,128]{2,1,0:T(8,128)(2,1)S(1)}, u32[]{:S(2)}, u32[]{:S(2)}) %collective-permute-start.12) | collective-permute-done | bytes 114720 | tf_op jit(solution)/shard_map/ppermute | solution.py:36
  39.0 0.8 %collective-permute-start.15 = (bf16[1,112,128]{2,1,0:T(8,128)(2,1)S(1)}, bf16[1,112,128]{2,1,0:T(8,128)(2,1)S(1)}, u32[]{:S(2)}, u32[]{:S(2)}) collective-permute-start(bf16[1,112,128]{2,1,0:T(8,128)(2,1)S(1)} %get-tuple-element.52.after), channel_id=1, source_target_pairs={{0,8},{2,10},{4,12},{6,14},{8,0},{10,2},{12,4},{14,6},{16,24},{18,... | collective-permute-start | bytes 86024 | tf_op jit(solution)/shard_map/ppermute | solution.py:36
  39.8 2.3 %collective-permute-start.16 = (bf16[1,112,128]{2,1,0:T(8,128)(2,1)S(1)}, bf16[1,112,128]{2,1,0:T(8,128)(2,1)S(1)}, u32[]{:S(2)}, u32[]{:S(2)}) collective-permute-start(bf16[1,112,128]{2,1,0:T(8,128)(2,1)S(1)} %get-tuple-element.55), channel_id=1, source_target_pairs={{0,16},{2,18},{4,20},{6,22},{8,24},{10,26},{12,28},{14,30},{16,0},... | collective-permute-start | bytes 86024 | tf_op jit(solution)/shard_map/ppermute | solution.py:36
  42.0 1.4 %collective-permute-start.17 = (bf16[1,112,128]{2,1,0:T(8,128)(2,1)S(1)}, bf16[1,112,128]{2,1,0:T(8,128)(2,1)S(1)}, u32[]{:S(2)}, u32[]{:S(2)}) collective-permute-start(bf16[1,112,128]{2,1,0:T(8,128)(2,1)S(1)} %get-tuple-element.56), channel_id=1, source_target_pairs={{0,24},{2,26},{4,28},{6,30},{8,16},{10,18},{12,20},{14,22},{16,8},... | collective-permute-start | bytes 86024 | tf_op jit(solution)/shard_map/ppermute | solution.py:36
  43.4 5.0 %shard_map.87 = (bf16[12,512,128]{2,1,0:T(8,128)(2,1)}, f32[8,128]{1,0:T(8,128)S(1)}) custom-call(s32[32]{0:T(128)S(1)} %copy-done.2, s32[12,27]{1,0:T(8,128)S(1)} %copy-done.1, f32[25,8,8,8,128]{4,3,2,1,0:T(8,128)S(1)} %get-tuple-element.36.field, f32[13,1,8,8,128]{4,3,2,1,0:T(8,128)S(1)} %get-tuple-element.40.low, ...), custom_call_target="tpu_custom_call" | custom-call | flops 2717908992 | bytes 1048576 | tf_op jit(solution)/shard_map/pallas_call | solution.py:573
  48.5 0.8 %shard_map.88 = f32[64,216]{1,0:T(8,128)} custom-call(f32[1,112,128]{2,1,0:T(8,128)S(1)} %get-tuple-element.54.held, bf16[1,112,128]{2,1,0:T(8,128)(2,1)S(1)} %collective-permute-done.15.refs_0_, bf16[1,112,128]{2,1,0:T(8,128)(2,1)S(1)} %collective-permute-done.16.refs_1_, bf16[1,112,128]{2,1,0:T(8,128)(2,1)S(1)} %collective-permute-done.17.refs_2_, ...), custom_call_target="tpu_custom_call" | custom-call | flops 1000000 | bytes 1048576 | tf_op jit(solution)/shard_map/pallas_call | solution.py:612
  (30 shorter events, 0.5 us)
Async XLA Ops:
  0.6 6.9 %copy-start = (bf16[216,64]{0,1:T(8,128)(2,1)S(1)}, bf16[216,64]{0,1:T(8,128)(2,1)}, u32[]{:S(2)}) copy-start(bf16[216,64]{0,1:T(8,128)(2,1)} %param.9) | copy-start | bytes 82948
  0.6 6.8 %collective-permute-start.1 = (bf16[1,64,216]{2,1,0:T(8,128)(2,1)}, bf16[1,64,216]{2,1,0:T(8,128)(2,1)S(1)}, u32[]{:S(2)}, u32[]{:S(2)}) collective-permute-start(bf16[1,64,216]{2,1,0:T(8,128)(2,1)} %bitcast.4), channel_id=1, source_target_pairs={{0,16},{2,18},{4,20},{6,22},{8,24},{10,26},{12,28},{14,30},{16,0},... | collective-permute-start | bytes 82952 | tf_op jit(solution)/shard_map/ppermute | solution.py:36
  7.5 2.2 %copy-start.1 = (s32[12,27]{1,0:T(8,128)S(1)}, s32[12,27]{1,0:T(8,128)}, u32[]{:S(2)}) copy-start(s32[12,27]{1,0:T(8,128)} %neighbors.7) | copy-start | bytes 3892
  7.5 8.8 %copy-start.2 = (s32[32]{0:T(128)S(1)}, s32[32]{0:T(128)}, u32[]{:S(2)}) copy-start(s32[32]{0:T(128)} %counts.7) | copy-start | bytes 388
  7.5 7.9 %collective-permute-start.2 = (bf16[12,512,128]{2,1,0:T(8,128)(2,1)S(1)}, bf16[12,512,128]{2,1,0:T(8,128)(2,1)S(1)}, u32[]{:S(2)}, u32[]{:S(2)}) collective-permute-start(bf16[12,512,128]{2,1,0:T(8,128)(2,1)S(1)} %get-tuple-element.33.acts), channel_id=1, source_target_pairs={{0,1},{1,0},{2,3},{3,2},{4,5},{5,4},{6,7},{7,6},{8,9},{9,8},{10,11... | collective-permute-start | bytes 4718600 | tf_op jit(solution)/shard_map/ppermute | solution.py:36
  7.6 8.7 %collective-permute-start.3 = (bf16[12,512,128]{2,1,0:T(8,128)(2,1)S(1)}, bf16[12,512,128]{2,1,0:T(8,128)(2,1)S(1)}, u32[]{:S(2)}, u32[]{:S(2)}) collective-permute-start(bf16[12,512,128]{2,1,0:T(8,128)(2,1)S(1)} %get-tuple-element.34.grads), channel_id=1, source_target_pairs={{0,1},{1,0},{2,3},{3,2},{4,5},{5,4},{6,7},{7,6},{8,9},{9,8},{10,11... | collective-permute-start | bytes 4718600 | tf_op jit(solution)/shard_map/ppermute | solution.py:36
  8.1 4.3 %collective-permute-start.4 = (bf16[2,64,216]{2,1,0:T(8,128)(2,1)S(1)}, bf16[2,64,216]{2,1,0:T(8,128)(2,1)S(1)}, u32[]{:S(2)}, u32[]{:S(2)}) collective-permute-start(bf16[2,64,216]{2,1,0:T(8,128)(2,1)S(1)} %get-tuple-element.35.refs_0_), channel_id=1, source_target_pairs={{0,8},{2,10},{4,12},{6,14},{8,0},{10,2},{12,4},{14,6},{16,24},{18,... | collective-permute-start | bytes 165896 | tf_op jit(solution)/shard_map/ppermute | solution.py:36
  9.7 4.3 %collective-permute-start = (s32[12,27]{1,0:T(8,128)S(1)}, s32[12,27]{1,0:T(8,128)S(1)}, u32[]{:S(2)}, u32[]{:S(2)}) collective-permute-start(s32[12,27]{1,0:T(8,128)S(1)} %copy-done.1), channel_id=1, source_target_pairs={{0,1},{1,0},{2,3},{3,2},{4,5},{5,4},{6,7},{7,6},{8,9},{9,8},{10,11... | collective-permute-start | bytes 3896 | tf_op jit(solution)/shard_map/ppermute | solution.py:36
  9.7 14.3 %collective-permute-start.5 = (bf16[12,64,128]{2,1,0:T(8,128)(2,1)S(1)}, bf16[12,64,128]{2,1,0:T(8,128)(2,1)S(1)}, u32[]{:S(2)}, u32[]{:S(2)}) collective-permute-start(bf16[12,64,128]{2,1,0:T(8,128)(2,1)S(1)} %get-tuple-element.37), channel_id=1, source_target_pairs={{1,2},{2,1},{3,4},{4,3},{5,6},{6,5},{7,8},{8,7},{9,10},{10,9},{11,... | collective-permute-start | bytes 589832 | tf_op jit(solution)/shard_map/ppermute | solution.py:31
  12.4 10.7 %collective-permute-start.6 = (bf16[4,64,216]{2,1,0:T(8,128)(2,1)S(1)}, bf16[4,64,216]{2,1,0:T(8,128)(2,1)S(1)}, u32[]{:S(2)}, u32[]{:S(2)}) collective-permute-start(bf16[4,64,216]{2,1,0:T(8,128)(2,1)S(1)} %shard_map.79.after.refs_0_), channel_id=1, source_target_pairs={{0,2},{2,0},{4,6},{6,4},{8,10},{10,8},{12,14},{14,12},{16,18},{18,... | collective-permute-start | bytes 331784 | tf_op jit(solution)/shard_map/ppermute | solution.py:36
  13.9 9.1 %collective-permute-start.7 = (bf16[4,64,216]{2,1,0:T(8,128)(2,1)S(1)}, bf16[4,64,216]{2,1,0:T(8,128)(2,1)S(1)}, u32[]{:S(2)}, u32[]{:S(2)}) collective-permute-start(bf16[4,64,216]{2,1,0:T(8,128)(2,1)S(1)} %shard_map.79.after.refs_0_), channel_id=1, source_target_pairs={{0,4},{2,6},{4,0},{6,2},{8,12},{10,14},{12,8},{14,10},{16,20},{18,... | collective-permute-start | bytes 331784 | tf_op jit(solution)/shard_map/ppermute | solution.py:36
  15.5 8.5 %collective-permute-start.8 = (bf16[4,64,216]{2,1,0:T(8,128)(2,1)S(1)}, bf16[4,64,216]{2,1,0:T(8,128)(2,1)S(1)}, u32[]{:S(2)}, u32[]{:S(2)}) collective-permute-start(bf16[4,64,216]{2,1,0:T(8,128)(2,1)S(1)} %shard_map.79.after.refs_0_), channel_id=1, source_target_pairs={{0,6},{2,4},{4,2},{6,0},{8,14},{10,12},{12,10},{14,8},{16,22},{18,... | collective-permute-start | bytes 331784 | tf_op jit(solution)/shard_map/ppermute | solution.py:36
  26.2 2.2 %collective-permute-start.10 = (bf16[2560,128]{1,0:T(8,128)(2,1)S(1)}, bf16[2560,128]{1,0:T(8,128)(2,1)S(1)}, u32[]{:S(2)}, u32[]{:S(2)}) collective-permute-start(bf16[2560,128]{1,0:T(8,128)(2,1)S(1)} %get-tuple-element.43), channel_id=1, source_target_pairs={{0,1},{1,0},{2,3},{3,2},{4,5},{5,4},{6,7},{7,6},{8,9},{9,8},{10,11... | collective-permute-start | bytes 1966088 | tf_op jit(solution)/shard_map/ppermute | solution.py:36
  26.3 6.7 %collective-permute-start.9 = (bf16[16,64,216]{2,1,0:T(8,128)(2,1)S(1)}, bf16[16,64,216]{2,1,0:T(8,128)(2,1)S(1)}, u32[]{:S(2)}, u32[]{:S(2)}) collective-permute-start(bf16[16,64,216]{2,1,0:T(8,128)(2,1)S(1)} %shard_map.81.after.held), channel_id=1, source_target_pairs={{0,1},{1,0},{2,3},{3,2},{4,5},{5,4},{6,7},{7,6},{8,9},{9,8},{10,11... | collective-permute-start | bytes 1327112 | tf_op jit(solution)/shard_map/ppermute | solution.py:36
  28.5 9.4 %collective-permute-start.11 = (bf16[4,112,128]{2,1,0:T(8,128)(2,1)S(1)}, bf16[4,112,128]{2,1,0:T(8,128)(2,1)S(1)}, u32[]{:S(2)}, u32[]{:S(2)}) collective-permute-start(bf16[4,112,128]{2,1,0:T(8,128)(2,1)S(1)} %get-tuple-element.44.after), channel_id=1, source_target_pairs={{0,2},{2,0},{4,6},{6,4},{8,10},{10,8},{12,14},{14,12},{16,18},{18,... | collective-permute-start | bytes 344072 | tf_op jit(solution)/shard_map/ppermute | solution.py:36
  31.5 7.4 %collective-permute-start.12 = (bf16[4,112,128]{2,1,0:T(8,128)(2,1)S(1)}, bf16[4,112,128]{2,1,0:T(8,128)(2,1)S(1)}, u32[]{:S(2)}, u32[]{:S(2)}) collective-permute-start(bf16[4,112,128]{2,1,0:T(8,128)(2,1)S(1)} %get-tuple-element.46), channel_id=1, source_target_pairs={{0,4},{2,6},{4,0},{6,2},{8,12},{10,14},{12,8},{14,10},{16,20},{18,... | collective-permute-start | bytes 344072 | tf_op jit(solution)/shard_map/ppermute | solution.py:36
  31.5 7.4 %collective-permute-start.13 = (bf16[4,112,128]{2,1,0:T(8,128)(2,1)S(1)}, bf16[4,112,128]{2,1,0:T(8,128)(2,1)S(1)}, u32[]{:S(2)}, u32[]{:S(2)}) collective-permute-start(bf16[4,112,128]{2,1,0:T(8,128)(2,1)S(1)} %get-tuple-element.47), channel_id=1, source_target_pairs={{0,6},{2,4},{4,2},{6,0},{8,14},{10,12},{12,10},{14,8},{16,22},{18,... | collective-permute-start | bytes 344072 | tf_op jit(solution)/shard_map/ppermute | solution.py:36
  38.9 4.5 %collective-permute-start.14 = (bf16[6,512,128]{2,1,0:T(8,128)(2,1)S(1)}, bf16[6,512,128]{2,1,0:T(8,128)(2,1)S(1)}, u32[]{:S(2)}, u32[]{:S(2)}) collective-permute-start(bf16[6,512,128]{2,1,0:T(8,128)(2,1)S(1)} %get-tuple-element.51.done), channel_id=1, source_target_pairs={{0,1},{1,0},{2,3},{3,2},{4,5},{5,4},{6,7},{7,6},{8,9},{9,8},{10,11... | collective-permute-start | bytes 2359304 | tf_op jit(solution)/shard_map/ppermute | solution.py:36
  39.0 9.5 %collective-permute-start.15 = (bf16[1,112,128]{2,1,0:T(8,128)(2,1)S(1)}, bf16[1,112,128]{2,1,0:T(8,128)(2,1)S(1)}, u32[]{:S(2)}, u32[]{:S(2)}) collective-permute-start(bf16[1,112,128]{2,1,0:T(8,128)(2,1)S(1)} %get-tuple-element.52.after), channel_id=1, source_target_pairs={{0,8},{2,10},{4,12},{6,14},{8,0},{10,2},{12,4},{14,6},{16,24},{18,... | collective-permute-start | bytes 86024 | tf_op jit(solution)/shard_map/ppermute | solution.py:36
  39.8 8.7 %collective-permute-start.16 = (bf16[1,112,128]{2,1,0:T(8,128)(2,1)S(1)}, bf16[1,112,128]{2,1,0:T(8,128)(2,1)S(1)}, u32[]{:S(2)}, u32[]{:S(2)}) collective-permute-start(bf16[1,112,128]{2,1,0:T(8,128)(2,1)S(1)} %get-tuple-element.55), channel_id=1, source_target_pairs={{0,16},{2,18},{4,20},{6,22},{8,24},{10,26},{12,28},{14,30},{16,0},... | collective-permute-start | bytes 86024 | tf_op jit(solution)/shard_map/ppermute | solution.py:36
  42.0 6.5 %collective-permute-start.17 = (bf16[1,112,128]{2,1,0:T(8,128)(2,1)S(1)}, bf16[1,112,128]{2,1,0:T(8,128)(2,1)S(1)}, u32[]{:S(2)}, u32[]{:S(2)}) collective-permute-start(bf16[1,112,128]{2,1,0:T(8,128)(2,1)S(1)} %get-tuple-element.56), channel_id=1, source_target_pairs={{0,24},{2,26},{4,28},{6,30},{8,16},{10,18},{12,20},{14,22},{16,8},... | collective-permute-start | bytes 86024 | tf_op jit(solution)/shard_map/ppermute | solution.py:36

commit v2 on v1

--- a/solution.py
+++ b/solution.py
@@ -286,7 +286,8 @@
 
 def stack_kernel(members, others, *refs):
     out = refs[members + others]
-    for member, ref in enumerate(refs[:members]):
+    for place, ref in enumerate(refs[:members]):
+        member = (members - place) % members
         for block in range(ref.shape[0]):
             out[block * members + member] = ref[block]
 
@@ -474,7 +475,7 @@
 
     def gather_start(number, own):
         unit, members = gather[number]
-        return [own] + [swapped(own, "space", unit * m) for m in range(1, members)]
+        return [own] + [swapped(own, "space", unit * m) for m in range(members - 1, 0, -1)]
 
     def gather_finish(arrived, after=(), passed=()):
         own = arrived[0]

time: 49.4 us -> 48.3 us (0.978); the launches traced: 49.3 us -> 47.7 us
  Pallas kernels: 22.7 us -> 19.6 us
  waiting for transfers between devices: 5.39 us -> 7.79 us
  starting transfers between devices: 20.4 us -> 19.5 us
    ppermute x17, waiting for transfers between devices: 5.39 us -> 7.78 us  [swapped(): return lax.ppermute(x, axis, [(i, i ^ mask) for i in range(count)])]
    pallas_call x1, Pallas kernels: 5.05 us -> 3.43 us  [input_rest(): call(functools.partial(input_rest_kernel, side), (like(acts.shape, bf16),...]
    pallas_call x1, Pallas kernels: 6.73 us -> 5.29 us  [on_device(): call(functools.partial(inner_kernel, side), (sums_shape, field_shape, lik...]
    ppermute x17, starting transfers between devices: 19.8 us -> 18.8 us  [swapped(): return lax.ppermute(x, axis, [(i, i ^ mask) for i in range(count)])]
  transfers between devices with their start and end apart: 18 -> 18, of which waited for: 4 -> 6; matrix products, arithmetic and copies ran while one was open for 0% -> 0% of each run, Pallas kernels for 40% -> 35%
where the time goes in v2:
time: 48.3 us; the launch traced here: 47.7 us
  Pallas kernels  19.6 us (41%)
  starting transfers between devices  19.5 us (40%)
  waiting for transfers between devices  7.79 us (16%)
  between operations  0.8 us (2%)
    ppermute x17, starting transfers between devices, swapped(): return lax.ppermute(x, axis, [(i, i ^ mask) for i in range(count)])  18.8 us
    ppermute x17, waiting for transfers between devices, swapped(): return lax.ppermute(x, axis, [(i, i ^ mask) for i in range(count)])  7.78 us
    pallas_call x1, Pallas kernels, on_device(): call(functools.partial(inner_kernel, side), (sums_shape, field_shape, lik...  5.29 us
    pallas_call x1, Pallas kernels, input_first(): call(functools.partial(input_first_kernel, side, spaces * padded), (like(...  4.41 us
    pallas_call x1, Pallas kernels, input_rest(): call(functools.partial(input_rest_kernel, side), (like(acts.shape, bf16),...  3.43 us
    pallas_call x1, Pallas kernels, on_device(): call(functools.partial(gate_kernel, side), (like(acts.shape, bf16), plane...  2.72 us
    pallas_call x1, Pallas kernels, on_device(): call(functools.partial(outer_kernel, side, rows, half), (like((spaces, pa...  2.24 us
  transfers between devices with their start and end apart: 18, of which 6 were waited for; matrix products, arithmetic and copies ran while one was open for 0% of the time, Pallas kernels for 35%

profile of v2, /device:TPU:0, one launch (start us, length us, event | category | flops | bytes accessed | tf_op | source)
XLA Modules:
  0.0 47.7 jit_solution(13463723631434030288)
XLA Ops:
  0.6 4.1 %collective-permute-start.1 = (bf16[1,64,216]{2,1,0:T(8,128)(2,1)}, bf16[1,64,216]{2,1,0:T(8,128)(2,1)S(1)}, u32[]{:S(2)}, u32[]{:S(2)}) collective-permute-start(bf16[1,64,216]{2,1,0:T(8,128)(2,1)} %bitcast.4), channel_id=1, source_target_pairs={{0,16},{2,18},{4,20},{6,22},{8,24},{10,26},{12,28},{14,30},{16,0},... | collective-permute-start | bytes 82952 | tf_op jit(solution)/shard_map/ppermute | solution.py:36
  4.7 2.7 %shard_map.77 = (bf16[12,512,128]{2,1,0:T(8,128)(2,1)S(1)}, bf16[12,64,128]{2,1,0:T(8,128)(2,1)S(1)}, bf16[12,64,128]{2,1,0:T(8,128)(2,1)S(1)}, bf16[12,512,128]{2,1,0:T(8,128)(2,1)S(1)}) custom-call(bf16[12,512,128]{2,1,0:T(8,128)(2,1)} %acts_far.1, bf16[12,512,128]{2,1,0:T(8,128)(2,1)} %preact_far.1, bf16[12,512,128]{2,1,0:T(8,128)(2,1)} %cotangent_far.1), custom_call_target="tpu_custom_call" | custom-call | flops 1087163648 | bytes 1048576 | tf_op jit(solution)/shard_map/pallas_call | solution.py:504
  8.1 1.6 %collective-permute-start.4 = (bf16[2,64,216]{2,1,0:T(8,128)(2,1)S(1)}, bf16[2,64,216]{2,1,0:T(8,128)(2,1)S(1)}, u32[]{:S(2)}, u32[]{:S(2)}) collective-permute-start(bf16[2,64,216]{2,1,0:T(8,128)(2,1)S(1)} %get-tuple-element.35.refs_0_), channel_id=1, source_target_pairs={{0,8},{2,10},{4,12},{6,14},{8,0},{10,2},{12,4},{14,6},{16,24},{18,... | collective-permute-start | bytes 165896 | tf_op jit(solution)/shard_map/ppermute | solution.py:36
  9.7 0.7 %collective-permute-start.5 = (bf16[12,64,128]{2,1,0:T(8,128)(2,1)S(1)}, bf16[12,64,128]{2,1,0:T(8,128)(2,1)S(1)}, u32[]{:S(2)}, u32[]{:S(2)}) collective-permute-start(bf16[12,64,128]{2,1,0:T(8,128)(2,1)S(1)} %get-tuple-element.37), channel_id=1, source_target_pairs={{1,2},{2,1},{3,4},{4,3},{5,6},{6,5},{7,8},{8,7},{9,10},{10,9},{11,... | collective-permute-start | bytes 589832 | tf_op jit(solution)/shard_map/ppermute | solution.py:31
  10.4 2.0 %collective-permute-done.4.refs_1_ = bf16[2,64,216]{2,1,0:T(8,128)(2,1)S(1)} collective-permute-done((bf16[2,64,216]{2,1,0:T(8,128)(2,1)S(1)}, bf16[2,64,216]{2,1,0:T(8,128)(2,1)S(1)}, u32[]{:S(2)}, u32[]{:S(2)}) %collective-permute-start.4) | collective-permute-done | bytes 55328 | tf_op jit(solution)/shard_map/ppermute | solution.py:36
  12.4 2.5 %collective-permute-start.6 = (bf16[4,64,216]{2,1,0:T(8,128)(2,1)S(1)}, bf16[4,64,216]{2,1,0:T(8,128)(2,1)S(1)}, u32[]{:S(2)}, u32[]{:S(2)}) collective-permute-start(bf16[4,64,216]{2,1,0:T(8,128)(2,1)S(1)} %shard_map.79.after.refs_0_), channel_id=1, source_target_pairs={{0,6},{2,4},{4,2},{6,0},{8,14},{10,12},{12,10},{14,8},{16,22},{18,... | collective-permute-start | bytes 331784 | tf_op jit(solution)/shard_map/ppermute | solution.py:36
  14.9 0.5 %collective-permute-start.7 = (bf16[4,64,216]{2,1,0:T(8,128)(2,1)S(1)}, bf16[4,64,216]{2,1,0:T(8,128)(2,1)S(1)}, u32[]{:S(2)}, u32[]{:S(2)}) collective-permute-start(bf16[4,64,216]{2,1,0:T(8,128)(2,1)S(1)} %shard_map.79.after.refs_0_), channel_id=1, source_target_pairs={{0,4},{2,6},{4,0},{6,2},{8,12},{10,14},{12,8},{14,10},{16,20},{18,... | collective-permute-start | bytes 331784 | tf_op jit(solution)/shard_map/ppermute | solution.py:36
  15.4 0.9 %collective-permute-start.8 = (bf16[4,64,216]{2,1,0:T(8,128)(2,1)S(1)}, bf16[4,64,216]{2,1,0:T(8,128)(2,1)S(1)}, u32[]{:S(2)}, u32[]{:S(2)}) collective-permute-start(bf16[4,64,216]{2,1,0:T(8,128)(2,1)S(1)} %shard_map.79.after.refs_0_), channel_id=1, source_target_pairs={{0,2},{2,0},{4,6},{6,4},{8,10},{10,8},{12,14},{14,12},{16,18},{18,... | collective-permute-start | bytes 331784 | tf_op jit(solution)/shard_map/ppermute | solution.py:36
  16.3 5.3 %shard_map.80 = (f32[384,1152]{1,0:T(8,128)S(1)}, f32[25,8,8,8,128]{4,3,2,1,0:T(8,128)S(1)}, f32[8,128]{1,0:T(8,128)S(1)}) custom-call(s32[32]{0:T(128)S(1)} %copy-done.2, s32[12,27]{1,0:T(8,128)S(1)} %copy-done.1, s32[12,27]{1,0:T(8,128)S(1)} %collective-permute-done.other_neighbors, bf16[12,512,128]{2,1,0:T(8,128)(2,1)S(1)} %get-tuple-element.33.acts, ...), custom_call_target="tpu_custom_call" | custom-call | flops 5435817984 | bytes 1048576 | tf_op jit(solution)/shard_map/pallas_call | solution.py:518
  21.6 0.9 %collective-permute-done.6.refs_1_ = bf16[4,64,216]{2,1,0:T(8,128)(2,1)S(1)} collective-permute-done((bf16[4,64,216]{2,1,0:T(8,128)(2,1)S(1)}, bf16[4,64,216]{2,1,0:T(8,128)(2,1)S(1)}, u32[]{:S(2)}, u32[]{:S(2)}) %collective-permute-start.6) | collective-permute-done | bytes 110624 | tf_op jit(solution)/shard_map/ppermute | solution.py:36
  23.0 1.8 %collective-permute-done.8.refs_3_ = bf16[4,64,216]{2,1,0:T(8,128)(2,1)S(1)} collective-permute-done((bf16[4,64,216]{2,1,0:T(8,128)(2,1)S(1)}, bf16[4,64,216]{2,1,0:T(8,128)(2,1)S(1)}, u32[]{:S(2)}, u32[]{:S(2)}) %collective-permute-start.8) | collective-permute-done | bytes 110624 | tf_op jit(solution)/shard_map/ppermute | solution.py:36
  24.9 2.2 %shard_map.82 = (f32[16,112,128]{2,1,0:T(8,128)S(1)}, bf16[2560,128]{1,0:T(8,128)(2,1)S(1)}, f32[13,1,8,8,128]{4,3,2,1,0:T(8,128)S(1)}, f32[13,1,8,8,128]{4,3,2,1,0:T(8,128)S(1)}) custom-call(s32[32]{0:T(128)S(1)} %copy-done.2, s32[12,27]{1,0:T(8,128)S(1)} %copy-done.1, bf16[12,512,128]{2,1,0:T(8,128)(2,1)S(1)} %get-tuple-element.33.acts, ...), custom_call_target="tpu_custom_call" | custom-call | flops 1087163648 | bytes 1048576 | tf_op jit(solution)/shard_map/pallas_call | solution.py:528
  27.7 1.6 %collective-permute-done.10.refs_0_.arrived = bf16[2560,128]{1,0:T(8,128)(2,1)S(1)} collective-permute-done((bf16[2560,128]{1,0:T(8,128)(2,1)S(1)}, bf16[2560,128]{1,0:T(8,128)(2,1)S(1)}, u32[]{:S(2)}, u32[]{:S(2)}) %collective-permute-start.10) | collective-permute-done | bytes 655392 | tf_op jit(solution)/shard_map/ppermute | solution.py:36
  29.4 1.1 %collective-permute-start.11 = (bf16[4,112,128]{2,1,0:T(8,128)(2,1)S(1)}, bf16[4,112,128]{2,1,0:T(8,128)(2,1)S(1)}, u32[]{:S(2)}, u32[]{:S(2)}) collective-permute-start(bf16[4,112,128]{2,1,0:T(8,128)(2,1)S(1)} %get-tuple-element.44.after), channel_id=1, source_target_pairs={{0,2},{2,0},{4,6},{6,4},{8,10},{10,8},{12,14},{14,12},{16,18},{18,... | collective-permute-start | bytes 344072 | tf_op jit(solution)/shard_map/ppermute | solution.py:36
  30.5 1.5 %collective-permute-start.12 = (bf16[4,112,128]{2,1,0:T(8,128)(2,1)S(1)}, bf16[4,112,128]{2,1,0:T(8,128)(2,1)S(1)}, u32[]{:S(2)}, u32[]{:S(2)}) collective-permute-start(bf16[4,112,128]{2,1,0:T(8,128)(2,1)S(1)} %get-tuple-element.46), channel_id=1, source_target_pairs={{0,4},{2,6},{4,0},{6,2},{8,12},{10,14},{12,8},{14,10},{16,20},{18,... | collective-permute-start | bytes 344072 | tf_op jit(solution)/shard_map/ppermute | solution.py:36
  32.1 0.9 %collective-permute-start.13 = (bf16[4,112,128]{2,1,0:T(8,128)(2,1)S(1)}, bf16[4,112,128]{2,1,0:T(8,128)(2,1)S(1)}, u32[]{:S(2)}, u32[]{:S(2)}) collective-permute-start(bf16[4,112,128]{2,1,0:T(8,128)(2,1)S(1)} %get-tuple-element.47), channel_id=1, source_target_pairs={{0,6},{2,4},{4,2},{6,0},{8,14},{10,12},{12,10},{14,8},{16,22},{18,... | collective-permute-start | bytes 344072 | tf_op jit(solution)/shard_map/ppermute | solution.py:36
  33.0 0.5 %shard_map.84.filt = bf16[1152,384]{1,0:T(8,128)(2,1)S(1)} custom-call(bf16[16,64,216]{2,1,0:T(8,128)(2,1)S(1)} %shard_map.81.after.held, bf16[16,64,216]{2,1,0:T(8,128)(2,1)S(1)} %collective-permute-done.9.arrived, bf16[4,112,128]{2,1,0:T(8,128)(2,1)S(1)} %get-tuple-element.44.after), custom_call_target="tpu_custom_call" | custom-call | flops 1000000 | bytes 1048576 | tf_op jit(solution)/shard_map/pallas_call | solution.py:546
  33.5 4.4 %shard_map.85 = (bf16[6,512,128]{2,1,0:T(8,128)(2,1)S(1)}, f32[8,128]{1,0:T(8,128)S(1)}) custom-call(s32[32]{0:T(128)S(1)} %copy-done.2, s32[12,27]{1,0:T(8,128)S(1)} %copy-done.1, s32[12,27]{1,0:T(8,128)S(1)} %collective-permute-done.other_neighbors, f32[25,8,8,8,128]{4,3,2,1,0:T(8,128)S(1)} %get-tuple-element.36.field, ...), custom_call_target="tpu_custom_call" | custom-call | flops 2717908992 | bytes 1048576 | tf_op jit(solution)/shard_map/pallas_call | solution.py:562
  38.1 0.9 %collective-permute-start.15 = (bf16[1,112,128]{2,1,0:T(8,128)(2,1)S(1)}, bf16[1,112,128]{2,1,0:T(8,128)(2,1)S(1)}, u32[]{:S(2)}, u32[]{:S(2)}) collective-permute-start(bf16[1,112,128]{2,1,0:T(8,128)(2,1)S(1)} %get-tuple-element.52.after), channel_id=1, source_target_pairs={{0,8},{2,10},{4,12},{6,14},{8,0},{10,2},{12,4},{14,6},{16,24},{18,... | collective-permute-start | bytes 86024 | tf_op jit(solution)/shard_map/ppermute | solution.py:36
  39.0 2.2 %collective-permute-start.16 = (bf16[1,112,128]{2,1,0:T(8,128)(2,1)S(1)}, bf16[1,112,128]{2,1,0:T(8,128)(2,1)S(1)}, u32[]{:S(2)}, u32[]{:S(2)}) collective-permute-start(bf16[1,112,128]{2,1,0:T(8,128)(2,1)S(1)} %get-tuple-element.55), channel_id=1, source_target_pairs={{0,16},{2,18},{4,20},{6,22},{8,24},{10,26},{12,28},{14,30},{16,0},... | collective-permute-start | bytes 86024 | tf_op jit(solution)/shard_map/ppermute | solution.py:36
  41.2 1.3 %collective-permute-start.17 = (bf16[1,112,128]{2,1,0:T(8,128)(2,1)S(1)}, bf16[1,112,128]{2,1,0:T(8,128)(2,1)S(1)}, u32[]{:S(2)}, u32[]{:S(2)}) collective-permute-start(bf16[1,112,128]{2,1,0:T(8,128)(2,1)S(1)} %get-tuple-element.56), channel_id=1, source_target_pairs={{0,24},{2,26},{4,28},{6,30},{8,16},{10,18},{12,20},{14,22},{16,8},... | collective-permute-start | bytes 86024 | tf_op jit(solution)/shard_map/ppermute | solution.py:36
  42.5 3.4 %shard_map.87 = (bf16[12,512,128]{2,1,0:T(8,128)(2,1)}, f32[8,128]{1,0:T(8,128)S(1)}) custom-call(s32[32]{0:T(128)S(1)} %copy-done.2, s32[12,27]{1,0:T(8,128)S(1)} %copy-done.1, f32[25,8,8,8,128]{4,3,2,1,0:T(8,128)S(1)} %get-tuple-element.36.field, f32[13,1,8,8,128]{4,3,2,1,0:T(8,128)S(1)} %get-tuple-element.40.low, ...), custom_call_target="tpu_custom_call" | custom-call | flops 2717908992 | bytes 1048576 | tf_op jit(solution)/shard_map/pallas_call | solution.py:574
  46.0 0.9 %collective-permute-done.17.refs_2_ = bf16[1,112,128]{2,1,0:T(8,128)(2,1)S(1)} collective-permute-done((bf16[1,112,128]{2,1,0:T(8,128)(2,1)S(1)}, bf16[1,112,128]{2,1,0:T(8,128)(2,1)S(1)}, u32[]{:S(2)}, u32[]{:S(2)}) %collective-permute-start.17) | collective-permute-done | bytes 28704 | tf_op jit(solution)/shard_map/ppermute | solution.py:36
  46.9 0.8 %shard_map.88 = f32[64,216]{1,0:T(8,128)} custom-call(f32[1,112,128]{2,1,0:T(8,128)S(1)} %get-tuple-element.54.held, bf16[1,112,128]{2,1,0:T(8,128)(2,1)S(1)} %collective-permute-done.15.refs_0_, bf16[1,112,128]{2,1,0:T(8,128)(2,1)S(1)} %collective-permute-done.16.refs_1_, bf16[1,112,128]{2,1,0:T(8,128)(2,1)S(1)} %collective-permute-done.17.refs_2_, ...), custom_call_target="tpu_custom_call" | custom-call | flops 1000000 | bytes 1048576 | tf_op jit(solution)/shard_map/pallas_call | solution.py:613
  (30 shorter events, 2.0 us)
Async XLA Ops:
  0.6 6.9 %copy-start = (bf16[216,64]{0,1:T(8,128)(2,1)S(1)}, bf16[216,64]{0,1:T(8,128)(2,1)}, u32[]{:S(2)}) copy-start(bf16[216,64]{0,1:T(8,128)(2,1)} %param.9) | copy-start | bytes 82948
  0.6 6.8 %collective-permute-start.1 = (bf16[1,64,216]{2,1,0:T(8,128)(2,1)}, bf16[1,64,216]{2,1,0:T(8,128)(2,1)S(1)}, u32[]{:S(2)}, u32[]{:S(2)}) collective-permute-start(bf16[1,64,216]{2,1,0:T(8,128)(2,1)} %bitcast.4), channel_id=1, source_target_pairs={{0,16},{2,18},{4,20},{6,22},{8,24},{10,26},{12,28},{14,30},{16,0},... | collective-permute-start | bytes 82952 | tf_op jit(solution)/shard_map/ppermute | solution.py:36
  7.5 2.2 %copy-start.1 = (s32[12,27]{1,0:T(8,128)S(1)}, s32[12,27]{1,0:T(8,128)}, u32[]{:S(2)}) copy-start(s32[12,27]{1,0:T(8,128)} %neighbors.7) | copy-start | bytes 3892
  7.5 8.8 %copy-start.2 = (s32[32]{0:T(128)S(1)}, s32[32]{0:T(128)}, u32[]{:S(2)}) copy-start(s32[32]{0:T(128)} %counts.7) | copy-start | bytes 388
  7.5 7.9 %collective-permute-start.2 = (bf16[12,512,128]{2,1,0:T(8,128)(2,1)S(1)}, bf16[12,512,128]{2,1,0:T(8,128)(2,1)S(1)}, u32[]{:S(2)}, u32[]{:S(2)}) collective-permute-start(bf16[12,512,128]{2,1,0:T(8,128)(2,1)S(1)} %get-tuple-element.33.acts), channel_id=1, source_target_pairs={{0,1},{1,0},{2,3},{3,2},{4,5},{5,4},{6,7},{7,6},{8,9},{9,8},{10,11... | collective-permute-start | bytes 4718600 | tf_op jit(solution)/shard_map/ppermute | solution.py:36
  7.6 8.7 %collective-permute-start.3 = (bf16[12,512,128]{2,1,0:T(8,128)(2,1)S(1)}, bf16[12,512,128]{2,1,0:T(8,128)(2,1)S(1)}, u32[]{:S(2)}, u32[]{:S(2)}) collective-permute-start(bf16[12,512,128]{2,1,0:T(8,128)(2,1)S(1)} %get-tuple-element.34.grads), channel_id=1, source_target_pairs={{0,1},{1,0},{2,3},{3,2},{4,5},{5,4},{6,7},{7,6},{8,9},{9,8},{10,11... | collective-permute-start | bytes 4718600 | tf_op jit(solution)/shard_map/ppermute | solution.py:36
  8.1 4.3 %collective-permute-start.4 = (bf16[2,64,216]{2,1,0:T(8,128)(2,1)S(1)}, bf16[2,64,216]{2,1,0:T(8,128)(2,1)S(1)}, u32[]{:S(2)}, u32[]{:S(2)}) collective-permute-start(bf16[2,64,216]{2,1,0:T(8,128)(2,1)S(1)} %get-tuple-element.35.refs_0_), channel_id=1, source_target_pairs={{0,8},{2,10},{4,12},{6,14},{8,0},{10,2},{12,4},{14,6},{16,24},{18,... | collective-permute-start | bytes 165896 | tf_op jit(solution)/shard_map/ppermute | solution.py:36
  9.7 5.2 %collective-permute-start = (s32[12,27]{1,0:T(8,128)S(1)}, s32[12,27]{1,0:T(8,128)S(1)}, u32[]{:S(2)}, u32[]{:S(2)}) collective-permute-start(s32[12,27]{1,0:T(8,128)S(1)} %copy-done.1), channel_id=1, source_target_pairs={{0,1},{1,0},{2,3},{3,2},{4,5},{5,4},{6,7},{7,6},{8,9},{9,8},{10,11... | collective-permute-start | bytes 3896 | tf_op jit(solution)/shard_map/ppermute | solution.py:36
  9.7 15.2 %collective-permute-start.5 = (bf16[12,64,128]{2,1,0:T(8,128)(2,1)S(1)}, bf16[12,64,128]{2,1,0:T(8,128)(2,1)S(1)}, u32[]{:S(2)}, u32[]{:S(2)}) collective-permute-start(bf16[12,64,128]{2,1,0:T(8,128)(2,1)S(1)} %get-tuple-element.37), channel_id=1, source_target_pairs={{1,2},{2,1},{3,4},{4,3},{5,6},{6,5},{7,8},{8,7},{9,10},{10,9},{11,... | collective-permute-start | bytes 589832 | tf_op jit(solution)/shard_map/ppermute | solution.py:31
  12.4 10.1 %collective-permute-start.6 = (bf16[4,64,216]{2,1,0:T(8,128)(2,1)S(1)}, bf16[4,64,216]{2,1,0:T(8,128)(2,1)S(1)}, u32[]{:S(2)}, u32[]{:S(2)}) collective-permute-start(bf16[4,64,216]{2,1,0:T(8,128)(2,1)S(1)} %shard_map.79.after.refs_0_), channel_id=1, source_target_pairs={{0,6},{2,4},{4,2},{6,0},{8,14},{10,12},{12,10},{14,8},{16,22},{18,... | collective-permute-start | bytes 331784 | tf_op jit(solution)/shard_map/ppermute | solution.py:36
  14.9 8.1 %collective-permute-start.7 = (bf16[4,64,216]{2,1,0:T(8,128)(2,1)S(1)}, bf16[4,64,216]{2,1,0:T(8,128)(2,1)S(1)}, u32[]{:S(2)}, u32[]{:S(2)}) collective-permute-start(bf16[4,64,216]{2,1,0:T(8,128)(2,1)S(1)} %shard_map.79.after.refs_0_), channel_id=1, source_target_pairs={{0,4},{2,6},{4,0},{6,2},{8,12},{10,14},{12,8},{14,10},{16,20},{18,... | collective-permute-start | bytes 331784 | tf_op jit(solution)/shard_map/ppermute | solution.py:36
  15.4 9.4 %collective-permute-start.8 = (bf16[4,64,216]{2,1,0:T(8,128)(2,1)S(1)}, bf16[4,64,216]{2,1,0:T(8,128)(2,1)S(1)}, u32[]{:S(2)}, u32[]{:S(2)}) collective-permute-start(bf16[4,64,216]{2,1,0:T(8,128)(2,1)S(1)} %shard_map.79.after.refs_0_), channel_id=1, source_target_pairs={{0,2},{2,0},{4,6},{6,4},{8,10},{10,8},{12,14},{14,12},{16,18},{18,... | collective-permute-start | bytes 331784 | tf_op jit(solution)/shard_map/ppermute | solution.py:36
  27.1 2.2 %collective-permute-start.10 = (bf16[2560,128]{1,0:T(8,128)(2,1)S(1)}, bf16[2560,128]{1,0:T(8,128)(2,1)S(1)}, u32[]{:S(2)}, u32[]{:S(2)}) collective-permute-start(bf16[2560,128]{1,0:T(8,128)(2,1)S(1)} %get-tuple-element.43), channel_id=1, source_target_pairs={{0,1},{1,0},{2,3},{3,2},{4,5},{5,4},{6,7},{7,6},{8,9},{9,8},{10,11... | collective-permute-start | bytes 1966088 | tf_op jit(solution)/shard_map/ppermute | solution.py:36
  27.3 5.6 %collective-permute-start.9 = (bf16[16,64,216]{2,1,0:T(8,128)(2,1)S(1)}, bf16[16,64,216]{2,1,0:T(8,128)(2,1)S(1)}, u32[]{:S(2)}, u32[]{:S(2)}) collective-permute-start(bf16[16,64,216]{2,1,0:T(8,128)(2,1)S(1)} %shard_map.81.after.held), channel_id=1, source_target_pairs={{0,1},{1,0},{2,3},{3,2},{4,5},{5,4},{6,7},{7,6},{8,9},{9,8},{10,11... | collective-permute-start | bytes 1327112 | tf_op jit(solution)/shard_map/ppermute | solution.py:36
  29.4 8.5 %collective-permute-start.11 = (bf16[4,112,128]{2,1,0:T(8,128)(2,1)S(1)}, bf16[4,112,128]{2,1,0:T(8,128)(2,1)S(1)}, u32[]{:S(2)}, u32[]{:S(2)}) collective-permute-start(bf16[4,112,128]{2,1,0:T(8,128)(2,1)S(1)} %get-tuple-element.44.after), channel_id=1, source_target_pairs={{0,2},{2,0},{4,6},{6,4},{8,10},{10,8},{12,14},{14,12},{16,18},{18,... | collective-permute-start | bytes 344072 | tf_op jit(solution)/shard_map/ppermute | solution.py:36
  30.5 7.4 %collective-permute-start.12 = (bf16[4,112,128]{2,1,0:T(8,128)(2,1)S(1)}, bf16[4,112,128]{2,1,0:T(8,128)(2,1)S(1)}, u32[]{:S(2)}, u32[]{:S(2)}) collective-permute-start(bf16[4,112,128]{2,1,0:T(8,128)(2,1)S(1)} %get-tuple-element.46), channel_id=1, source_target_pairs={{0,4},{2,6},{4,0},{6,2},{8,12},{10,14},{12,8},{14,10},{16,20},{18,... | collective-permute-start | bytes 344072 | tf_op jit(solution)/shard_map/ppermute | solution.py:36
  32.1 5.9 %collective-permute-start.13 = (bf16[4,112,128]{2,1,0:T(8,128)(2,1)S(1)}, bf16[4,112,128]{2,1,0:T(8,128)(2,1)S(1)}, u32[]{:S(2)}, u32[]{:S(2)}) collective-permute-start(bf16[4,112,128]{2,1,0:T(8,128)(2,1)S(1)} %get-tuple-element.47), channel_id=1, source_target_pairs={{0,6},{2,4},{4,2},{6,0},{8,14},{10,12},{12,10},{14,8},{16,22},{18,... | collective-permute-start | bytes 344072 | tf_op jit(solution)/shard_map/ppermute | solution.py:36
  38.0 4.6 %collective-permute-start.14 = (bf16[6,512,128]{2,1,0:T(8,128)(2,1)S(1)}, bf16[6,512,128]{2,1,0:T(8,128)(2,1)S(1)}, u32[]{:S(2)}, u32[]{:S(2)}) collective-permute-start(bf16[6,512,128]{2,1,0:T(8,128)(2,1)S(1)} %get-tuple-element.51.done), channel_id=1, source_target_pairs={{0,1},{1,0},{2,3},{3,2},{4,5},{5,4},{6,7},{7,6},{8,9},{9,8},{10,11... | collective-permute-start | bytes 2359304 | tf_op jit(solution)/shard_map/ppermute | solution.py:36
  38.1 7.9 %collective-permute-start.15 = (bf16[1,112,128]{2,1,0:T(8,128)(2,1)S(1)}, bf16[1,112,128]{2,1,0:T(8,128)(2,1)S(1)}, u32[]{:S(2)}, u32[]{:S(2)}) collective-permute-start(bf16[1,112,128]{2,1,0:T(8,128)(2,1)S(1)} %get-tuple-element.52.after), channel_id=1, source_target_pairs={{0,8},{2,10},{4,12},{6,14},{8,0},{10,2},{12,4},{14,6},{16,24},{18,... | collective-permute-start | bytes 86024 | tf_op jit(solution)/shard_map/ppermute | solution.py:36
  39.0 7.0 %collective-permute-start.16 = (bf16[1,112,128]{2,1,0:T(8,128)(2,1)S(1)}, bf16[1,112,128]{2,1,0:T(8,128)(2,1)S(1)}, u32[]{:S(2)}, u32[]{:S(2)}) collective-permute-start(bf16[1,112,128]{2,1,0:T(8,128)(2,1)S(1)} %get-tuple-element.55), channel_id=1, source_target_pairs={{0,16},{2,18},{4,20},{6,22},{8,24},{10,26},{12,28},{14,30},{16,0},... | collective-permute-start | bytes 86024 | tf_op jit(solution)/shard_map/ppermute | solution.py:36
  41.2 5.7 %collective-permute-start.17 = (bf16[1,112,128]{2,1,0:T(8,128)(2,1)S(1)}, bf16[1,112,128]{2,1,0:T(8,128)(2,1)S(1)}, u32[]{:S(2)}, u32[]{:S(2)}) collective-permute-start(bf16[1,112,128]{2,1,0:T(8,128)(2,1)S(1)} %get-tuple-element.56), channel_id=1, source_target_pairs={{0,24},{2,26},{4,28},{6,30},{8,16},{10,18},{12,20},{14,22},{16,8},... | collective-permute-start | bytes 86024 | tf_op jit(solution)/shard_map/ppermute | solution.py:36
